TPU v7x, 32 devices: a whole 2x2x4 slice. The times are simulated.
32 devices in a mesh: ctx: 8 (over z, y), head: 4 (over x, core).
Axes of the slice: x: 2, y: 2, z: 4, core: 2. Of those that a mesh axis runs over, the one named last changes fastest.
Arguments:
- tokens: bfloat16 [4096, 2048], P('ctx'), may hold values from -6 to 6
- w_proj: bfloat16 [2048, 10240], P('ctx', 'head'), may hold values from -0.125 to 0.125
- w_small: bfloat16 [2048, 48], P('ctx', 'head'), may hold values from -0.125 to 0.125
- beta_bias: float32 [16, 2], P('head'), may hold values from 5 to 9
- decay_rate: float32 [16], P('head'), may hold values from 5e-07 to 0.05
- w_out: bfloat16 [2048, 2048], P('head', 'ctx'), may hold values from -0.125 to 0.125
Outputs:
- mixed: bfloat16 [4096, 2048], P(('ctx', 'head'))
All inputs are finite; a program needn't handle non-finite values.
Results may differ from a plain program's by a relative error of at most 0.006.
Values may be sent and summed in bfloat16 or wider, within the bound.
A program may use at most 128 MiB of HBM per device.

v0:
```python
import math

import jax
import jax.numpy as jnp
from jax import lax
from jax.sharding import PartitionSpec as P

HIGHEST_PRECISION = lax.Precision.HIGHEST


def from_behind(array, axis, by):
    count = lax.axis_size(axis)
    pairs = [(i, i + by) for i in range(count) if 0 <= i + by < count]
    return lax.ppermute(array, axis, pairs)


def matrix_product(left, right):
    return jnp.matmul(left, right, precision=HIGHEST_PRECISION)


def unit_rows(vectors):
    return vectors / jnp.sqrt(jnp.sum(vectors * vectors, axis=-1, keepdims=True) + 1e-06)


def compose(earlier, later):
    return (matrix_product(earlier[0], later[0]), matrix_product(earlier[1], later[0]) + later[1])


def shards(tokens, w_proj, w_small, beta_bias, decay_rate, w_out):
    tok_rows = tokens.shape[0]
    heads_here = beta_bias.shape[0]
    mirrors = beta_bias.shape[1]
    head_width = w_proj.shape[1] // (heads_here * (1 + 2 * mirrors))
    projected = jnp.dot(
        tokens,
        lax.all_gather(w_proj, "ctx", axis=0, tiled=True),
        preferred_element_type=jnp.float32,
    )
    gate_inputs = jnp.dot(
        tokens,
        lax.all_gather(w_small, "ctx", axis=0, tiled=True),
        preferred_element_type=jnp.float32,
    )
    parts = projected.reshape(tok_rows, heads_here, 1 + 2 * mirrors, head_width)
    queries = unit_rows(parts[:, :, 0])
    keys_all = unit_rows(parts[:, :, 1 : 1 + mirrors])
    values_all = parts[:, :, 1 + mirrors :]
    gate_cols = gate_inputs.reshape(tok_rows, heads_here, mirrors + 1)
    betas = 2.0 * jax.nn.sigmoid(gate_cols[:, :, :mirrors] + beta_bias[None])
    log_decay = -decay_rate[None, :] * jax.nn.softplus(gate_cols[:, :, mirrors])
    log_steps = jnp.concatenate(
        [log_decay[:, :, None], jnp.zeros((tok_rows, heads_here, mirrors - 1), jnp.float32)], axis=2
    )
    block_tok = math.gcd(tok_rows, 64)
    blocks = tok_rows // block_tok
    span = block_tok * mirrors

    def to_steps(array):
        moved = jnp.moveaxis(array, 1, 0)
        return moved.reshape((heads_here, blocks, span) + array.shape[3:])

    key_steps = to_steps(keys_all)
    value_steps = to_steps(values_all)
    beta_steps = to_steps(betas)
    running = jnp.cumsum(to_steps(log_steps), axis=-1)
    running_query = running[..., mirrors - 1 :: mirrors]
    query_blocks = jnp.moveaxis(queries, 1, 0).reshape(heads_here, blocks, block_tok, head_width)
    step_index = lax.iota(jnp.int32, span)
    strict = step_index[:, None] > step_index[None, :]
    inner = jnp.einsum("hnsk,hnrk->hnsr", key_steps, key_steps, precision=HIGHEST_PRECISION)
    spread = jnp.where(strict, running[..., :, None] - running[..., None, :], 0.0)
    lower_part = jnp.where(strict, beta_steps[..., :, None] * jnp.exp(spread) * inner, 0.0)
    system = lower_part + jnp.eye(span, dtype=jnp.float32)
    weighted_values = lax.linalg.triangular_solve(
        system, beta_steps[..., None] * value_steps, left_side=True, lower=True
    )
    weighted_keys = lax.linalg.triangular_solve(
        system, (beta_steps * jnp.exp(running))[..., None] * key_steps, left_side=True, lower=True
    )
    tail = jnp.exp(running[..., -1:] - running)
    identity_block = jnp.eye(head_width, dtype=jnp.float32)
    transitions = jnp.exp(running[..., -1])[..., None, None] * identity_block - jnp.einsum(
        "hnsa,hnsb->hnab", weighted_keys * tail[..., None], key_steps, precision=HIGHEST_PRECISION
    )
    writes = jnp.einsum(
        "hnsa,hnsb->hnab", weighted_values * tail[..., None], key_steps, precision=HIGHEST_PRECISION
    )
    inclusive = lax.associative_scan(compose, (transitions, writes), axis=1)
    square_shape = (heads_here, 1, head_width, head_width)
    start_trans = jnp.concatenate(
        [jnp.broadcast_to(identity_block, square_shape), inclusive[0][:, :-1]], axis=1
    )
    start_write = jnp.concatenate(
        [jnp.zeros(square_shape, jnp.float32), inclusive[1][:, :-1]], axis=1
    )
    device_trans = inclusive[0][:, -1]
    device_write = inclusive[1][:, -1]

    def relay(turn, incoming):
        outgoing = matrix_product(incoming, device_trans) + device_write
        return from_behind(outgoing, "ctx", 1)

    state_in = lax.fori_loop(
        0, lax.axis_size("ctx") - 1, relay, jnp.zeros(device_write.shape, jnp.float32)
    )
    states = (
        jnp.einsum("hab,hnbc->hnac", state_in, start_trans, precision=HIGHEST_PRECISION)
        + start_write
    )
    pseudo = weighted_values - jnp.einsum(
        "hnsb,hnab->hnsa", weighted_keys, states, precision=HIGHEST_PRECISION
    )
    token_index = lax.iota(jnp.int32, block_tok)
    visible = step_index[None, :] <= token_index[:, None] * mirrors + mirrors - 1
    scores = jnp.einsum("hntb,hnsb->hnts", query_blocks, key_steps, precision=HIGHEST_PRECISION)
    reach = jnp.where(visible, running_query[..., :, None] - running[..., None, :], 0.0)
    attend = jnp.where(visible, jnp.exp(reach) * scores, 0.0)
    head_out = jnp.exp(running_query)[..., None] * jnp.einsum(
        "hntb,hnab->hnta", query_blocks, states, precision=HIGHEST_PRECISION
    )
    head_out = head_out + jnp.einsum("hnts,hnsa->hnta", attend, pseudo, precision=HIGHEST_PRECISION)
    normed = head_out / jnp.sqrt(jnp.mean(head_out * head_out, axis=-1, keepdims=True) + 1e-06)
    mixed_heads = jnp.moveaxis(normed.reshape(heads_here, tok_rows, head_width), 0, 1)
    mixed_heads = mixed_heads.reshape(tok_rows, heads_here * head_width).astype(jnp.bfloat16)
    grouped = lax.all_gather(w_out, "head", axis=0, tiled=True)
    full_out = lax.all_gather(grouped, "ctx", axis=1, tiled=True)
    group_count = lax.axis_size("head")
    rows_each = tok_rows // group_count
    stacked = mixed_heads.reshape(group_count, rows_each, heads_here * head_width)
    mixed = jnp.einsum(
        "irk,kd->ird",
        lax.all_to_all(stacked, "head", split_axis=0, concat_axis=2, tiled=True),
        full_out,
        preferred_element_type=jnp.float32,
    ).astype(jnp.bfloat16)
    mixed = mixed.reshape(rows_each, full_out.shape[1])
    return mixed


def solution(mesh):
    placed = (
        P("ctx", None),
        P("ctx", "head"),
        P("ctx", "head"),
        P("head", None),
        P("head"),
        P("head", "ctx"),
    )
    return jax.shard_map(
        shards, mesh=mesh, in_specs=placed, out_specs=P(("ctx", "head"), None), check_vma=False
    )
```

profile of v0, /device:TPU:28, one launch (start us, length us, event | category | flops | bytes accessed | tf_op | source)
XLA Modules:
  0.0 764.5 jit_solution(7593181156184183211)
XLA Ops:
  6.5 0.7 all-gather.6.cloned.1.call-update
  8.1 30.7 %all_gather.12 = bf16[2048,12]{0,1:T(8,128)(2,1)S(1)} all-gather(bf16[256,12]{0,1:T(8,128)(2,1)} %param.12), channel_id=1, replica_groups=mesh['ctx'=8,'head'=4] {'ctx'}, dimensions={0}, use_global_device_ids=true | all-gather | bytes 55296 | tf_op jit(solution)/shard_map/all_gather | solution.py:41
  40.7 1.1 reduce_window_sum.11
  43.2 133.5 %all-gather.4.cloned.1.call-done = bf16[2048,2560]{1,0:T(8,128)(2,1)} async-done(((bf16[256,2560]{1,0:T(8,128)(2,1)}), bf16[2048,2560]{1,0:T(8,128)(2,1)}) %all-gather.4.cloned.1.call-update) | async-done | bytes 10485776 | tf_op jit(solution)/shard_map/all_gather | solution.py:36
  176.7 8.5 %fusion.64 = f32[512,2560]{0,1:T(8,128)S(1)} fusion(bf16[512,2048]{1,0:T(8,128)(2,1)S(1)} %copy-done, bf16[2048,2560]{1,0:T(8,128)(2,1)} %all-gather.4.cloned.1.call-done), kind=kOutput, calls=%fused_computation.110 | convolution fusion | flops 5368709120 | bytes 17825792 | tf_op jit(solution)/shard_map/dot_general | solution.py:34
  185.5 3.1 slice_bitcast_fusion
  189.0 2.9 copy.45
  191.9 5.9 select_bitcast_fusion
  197.7 316.1 %custom-call.4 = f32[4,8,1,128,128]{3,4,2,1,0:T(8,128)} custom-call(f32[4,8,1,128,128]{4,3,2,1,0:T(8,128)} %select_bitcast_fusion), custom_call_target="InvertDiagBlocksLowerTriangular" | custom-call | tf_op jit(solution)/shard_map/triangular_solve/custom-call.1 | solution.py:77
  513.8 5.7 fusion.6
  519.5 4.3 multiply_subtract_fusion
  523.8 1.2 fusion.26
  525.9 0.8 copy-done.16
  527.5 3.5 pad.42
  531.1 3.6 pad.43
  534.7 1.7 add.150
  536.3 6.4 pad.45
  542.7 6.4 pad.114
  549.1 14.6 %copy.50 = f32[4,512,2,128]{3,2,1,0:T(2,128)} copy(f32[4,512,2,128]{1,3,2,0:T(8,128)} %get-tuple-element.37) | data formatting | bytes 4194304 | tf_op jit(solution)/shard_map/transpose | solution.py:59
  563.7 2.3 bitcast_multiply_fusion
  566.0 3.6 fusion.4
  569.7 4.2 fusion.10
  573.9 1.2 convolution_add_fusion.1
  577.4 0.8 pad_maximum_fusion.3
  578.2 5.8 pad.48
  584.1 1.8 pad_add_fusion
  585.8 5.7 pad.49
  591.5 2.7 add.157
  594.3 10.1 %pad.112 = f32[4,8,128,128]{3,2,1,0:T(8,128)} pad(f32[4,4,128,128]{3,2,1,0:T(8,128)} %add.157, f32[]{:T(128)} %constant.11.clone.1), padding=0_0_0x1_0_1x0_0_0x0_0_0 | pad | bytes 3145732
  604.4 2.5 convolution_add_fusion.2
  607.0 1.0 pad_maximum_fusion.1
  608.0 10.1 %pad.66 = f32[4,7,128,128]{3,2,1,0:T(8,128)} pad(f32[4,4,128,128]{3,2,1,0:T(8,128)} %pad_maximum_fusion.1, f32[]{:T(128)} %constant.11.clone.1), padding=0_0_0x0_0_1x0_0_0x0_0_0 | pad | bytes 2883588 | tf_op jit(solution)/shard_map/slice | solution.py:94
  618.1 10.2 %pad.50 = f32[4,8,128,128]{3,2,1,0:T(8,128)} pad(f32[4,4,128,128]{3,2,1,0:T(8,128)} %pad_maximum_fusion.1, f32[]{:T(128)} %constant.11.clone.1), padding=0_0_0x0_1_1x0_0_0x0_0_0 | pad | bytes 3145732 | tf_op jit(solution)/shard_map/pad | solution.py:88
  628.4 1.3 multiply_reduce_fusion.2
  629.7 2.4 divide_bitcast_fusion.1
  632.1 2.6 copy.41
  634.7 2.0 fusion.34
  636.8 6.5 pad.44
  643.3 1.0 add_bitcast_fusion.1
  644.3 1.1 add_bitcast_fusion
  645.3 3.8 slice_add_fusion.2
  649.1 1.4 slice_add_fusion
  650.6 69.2 %while.10 = (s32[]{:T(128)}, f32[4,128,128]{2,1,0:T(8,128)S(1)}, f32[4,128,128]{2,1,0:T(8,128)S(1)}, f32[4,128,128]{2,1,0:T(8,128)S(1)}, s32[]{:T(128)}) while((s32[]{:T(128)}, f32[4,128,128]{2,1,0:T(8,128)S(1)}, f32[4,128,128]{2,1,0:T(8,128)S(1)}, f32[4,128,128]{2,1,0:T(8,128)S(1)}, s32[]{:T(128)}) %tuple.23), condition=%wide.region_4.6_spmd, body=%wide.region_3.5_spmd.sunk | while | flops 100728832 | bytes 2097253 | solution.py:103
  651.0 1.3 collective-permute-start
  652.3 8.8 %collective-permute-done = f32[4,128,128]{2,1,0:T(8,128)S(1)} collective-permute-done((f32[4,128,128]{2,1,0:T(8,128)S(1)}, f32[4,128,128]{2,1,0:T(8,128)S(1)}, u32[]{:S(2)}, u32[]{:S(2)}) %collective-permute-start) | collective-permute-done | bytes 262176 | tf_op jit(solution)/shard_map/while/body/eval_jaxpr/ppermute | solution.py:14
  661.5 1.3 collective-permute-start
  662.8 8.8 %collective-permute-done = f32[4,128,128]{2,1,0:T(8,128)S(1)} collective-permute-done((f32[4,128,128]{2,1,0:T(8,128)S(1)}, f32[4,128,128]{2,1,0:T(8,128)S(1)}, u32[]{:S(2)}, u32[]{:S(2)}) %collective-permute-start) | collective-permute-done | bytes 262176 | tf_op jit(solution)/shard_map/while/body/eval_jaxpr/ppermute | solution.py:14
  672.1 1.3 collective-permute-start
  673.4 8.0 %collective-permute-done = f32[4,128,128]{2,1,0:T(8,128)S(1)} collective-permute-done((f32[4,128,128]{2,1,0:T(8,128)S(1)}, f32[4,128,128]{2,1,0:T(8,128)S(1)}, u32[]{:S(2)}, u32[]{:S(2)}) %collective-permute-start) | collective-permute-done | bytes 262176 | tf_op jit(solution)/shard_map/while/body/eval_jaxpr/ppermute | solution.py:14
  681.7 1.3 collective-permute-start
  683.0 7.6 collective-permute-done
  691.0 1.3 collective-permute-start
  692.3 7.9 %collective-permute-done = f32[4,128,128]{2,1,0:T(8,128)S(1)} collective-permute-done((f32[4,128,128]{2,1,0:T(8,128)S(1)}, f32[4,128,128]{2,1,0:T(8,128)S(1)}, u32[]{:S(2)}, u32[]{:S(2)}) %collective-permute-start) | collective-permute-done | bytes 262176 | tf_op jit(solution)/shard_map/while/body/eval_jaxpr/ppermute | solution.py:14
  700.6 1.3 collective-permute-start
  701.9 7.9 %collective-permute-done = f32[4,128,128]{2,1,0:T(8,128)S(1)} collective-permute-done((f32[4,128,128]{2,1,0:T(8,128)S(1)}, f32[4,128,128]{2,1,0:T(8,128)S(1)}, u32[]{:S(2)}, u32[]{:S(2)}) %collective-permute-start) | collective-permute-done | bytes 262176 | tf_op jit(solution)/shard_map/while/body/eval_jaxpr/ppermute | solution.py:14
  710.1 1.3 collective-permute-start
  711.4 8.1 %collective-permute-done = f32[4,128,128]{2,1,0:T(8,128)S(1)} collective-permute-done((f32[4,128,128]{2,1,0:T(8,128)S(1)}, f32[4,128,128]{2,1,0:T(8,128)S(1)}, u32[]{:S(2)}, u32[]{:S(2)}) %collective-permute-start) | collective-permute-done | bytes 262176 | tf_op jit(solution)/shard_map/while/body/eval_jaxpr/ppermute | solution.py:14
  719.8 4.1 bitcast_add_fusion
  724.0 4.2 convolution_multiply_fusion.1
  728.2 4.2 fusion.22
  732.4 4.5 fusion.65
  736.9 2.4 multiply_reduce_fusion.1
  740.3 11.4 %all_to_all.15 = bf16[4,128,512]{2,1,0:T(8,128)(2,1)S(1)} all-to-all(bf16[4,128,512]{2,1,0:T(8,128)(2,1)S(1)} %convert_element_type.33), channel_id=1, replica_groups=mesh['ctx'=8,'head'=4] {'head'}, dimensions={0} | all-to-all | bytes 1048576 | tf_op jit(solution)/shard_map/all_to_all | solution.py:132
  752.0 5.6 convolution_convert_fusion
  (104 shorter events, 12.7 us)
Async XLA Ops:
  6.5 32.2 %copy-start = (bf16[512,2048]{1,0:T(8,128)(2,1)S(1)}, bf16[512,2048]{1,0:T(8,128)(2,1)}, u32[]{:S(2)}) copy-start(bf16[512,2048]{1,0:T(8,128)(2,1)} %param.10) | copy-start | bytes 6291460
  6.5 32.9 %copy-start.20 = (f32[4,2]{0,1:T(2,128)S(1)}, f32[4,2]{0,1:T(2,128)}, u32[]{:S(2)}) copy-start(f32[4,2]{0,1:T(2,128)} %param.13) | copy-start | bytes 100
  6.5 35.8 %all-gather.6.cloned.1.call-start = ((), (), s32[]{:S(2)}) async-start(), calls=%async_computation.2 | async-start | bytes 1310720 | tf_op jit(solution)/shard_map/all_gather | solution.py:125
  7.3 32.9 %copy-start.21 = (f32[4]{0:T(128)S(1)}, f32[4]{0:T(128)}, u32[]{:S(2)}) copy-start(f32[4]{0:T(128)} %param.14) | copy-start | bytes 52
  7.3 169.5 %all-gather.4.cloned.1.call-start = ((), (), s32[]{:S(2)}) async-start(), calls=%async_computation.1 | async-start | bytes 11796480 | tf_op jit(solution)/shard_map/all_gather | solution.py:36
  8.0 743.9 %all-gather.8.cloned.1.call-start = ((), (), s32[]{:S(2)}) async-start(), calls=%async_computation.3 | async-start | bytes 9437184 | tf_op jit(solution)/shard_map/all_gather | solution.py:126
  185.2 3.7 copy-start.8
  519.5 4.4 copy-start.6
  523.8 1.4 copy-start.2
  525.0 2.4 copy-start.9
  525.8 0.8 copy-start.16
  563.7 2.4 copy-start.12
  569.7 4.2 copy-start.4
  569.7 4.2 copy-start.3
  573.9 1.4 copy-start.13
  573.9 2.0 copy-start.10
  575.1 1.5 copy-start.17
  576.6 0.8 copy-start.18
  604.4 2.5 slice-start.1
  632.1 4.6 slice-start
  645.3 3.8 copy-start.14
  645.3 3.8 copy-start.15
  651.0 10.1 %collective-permute-start = (f32[4,128,128]{2,1,0:T(8,128)S(1)}, f32[4,128,128]{2,1,0:T(8,128)S(1)}, u32[]{:S(2)}, u32[]{:S(2)}) collective-permute-start(f32[4,128,128]{2,1,0:T(8,128)S(1)} %convolution_add_fusion.5), channel_id=1, source_target_pairs={{0,4},{4,8},{8,12},{12,16},{16,20},{20,24},{24,28},{1,5},{5,9},{9,... | collective-permute-start | bytes 786440 | tf_op jit(solution)/shard_map/while/body/eval_jaxpr/ppermute | solution.py:14
  661.5 10.1 %collective-permute-start = (f32[4,128,128]{2,1,0:T(8,128)S(1)}, f32[4,128,128]{2,1,0:T(8,128)S(1)}, u32[]{:S(2)}, u32[]{:S(2)}) collective-permute-start(f32[4,128,128]{2,1,0:T(8,128)S(1)} %convolution_add_fusion.5), channel_id=1, source_target_pairs={{0,4},{4,8},{8,12},{12,16},{16,20},{20,24},{24,28},{1,5},{5,9},{9,... | collective-permute-start | bytes 786440 | tf_op jit(solution)/shard_map/while/body/eval_jaxpr/ppermute | solution.py:14
  672.1 9.3 %collective-permute-start = (f32[4,128,128]{2,1,0:T(8,128)S(1)}, f32[4,128,128]{2,1,0:T(8,128)S(1)}, u32[]{:S(2)}, u32[]{:S(2)}) collective-permute-start(f32[4,128,128]{2,1,0:T(8,128)S(1)} %convolution_add_fusion.5), channel_id=1, source_target_pairs={{0,4},{4,8},{8,12},{12,16},{16,20},{20,24},{24,28},{1,5},{5,9},{9,... | collective-permute-start | bytes 786440 | tf_op jit(solution)/shard_map/while/body/eval_jaxpr/ppermute | solution.py:14
  681.7 8.9 %collective-permute-start = (f32[4,128,128]{2,1,0:T(8,128)S(1)}, f32[4,128,128]{2,1,0:T(8,128)S(1)}, u32[]{:S(2)}, u32[]{:S(2)}) collective-permute-start(f32[4,128,128]{2,1,0:T(8,128)S(1)} %convolution_add_fusion.5), channel_id=1, source_target_pairs={{0,4},{4,8},{8,12},{12,16},{16,20},{20,24},{24,28},{1,5},{5,9},{9,... | collective-permute-start | bytes 786440 | tf_op jit(solution)/shard_map/while/body/eval_jaxpr/ppermute | solution.py:14
  691.0 9.2 %collective-permute-start = (f32[4,128,128]{2,1,0:T(8,128)S(1)}, f32[4,128,128]{2,1,0:T(8,128)S(1)}, u32[]{:S(2)}, u32[]{:S(2)}) collective-permute-start(f32[4,128,128]{2,1,0:T(8,128)S(1)} %convolution_add_fusion.5), channel_id=1, source_target_pairs={{0,4},{4,8},{8,12},{12,16},{16,20},{20,24},{24,28},{1,5},{5,9},{9,... | collective-permute-start | bytes 786440 | tf_op jit(solution)/shard_map/while/body/eval_jaxpr/ppermute | solution.py:14
  700.6 9.2 %collective-permute-start = (f32[4,128,128]{2,1,0:T(8,128)S(1)}, f32[4,128,128]{2,1,0:T(8,128)S(1)}, u32[]{:S(2)}, u32[]{:S(2)}) collective-permute-start(f32[4,128,128]{2,1,0:T(8,128)S(1)} %convolution_add_fusion.5), channel_id=1, source_target_pairs={{0,4},{4,8},{8,12},{12,16},{16,20},{20,24},{24,28},{1,5},{5,9},{9,... | collective-permute-start | bytes 786440 | tf_op jit(solution)/shard_map/while/body/eval_jaxpr/ppermute | solution.py:14
  710.1 9.4 %collective-permute-start = (f32[4,128,128]{2,1,0:T(8,128)S(1)}, f32[4,128,128]{2,1,0:T(8,128)S(1)}, u32[]{:S(2)}, u32[]{:S(2)}) collective-permute-start(f32[4,128,128]{2,1,0:T(8,128)S(1)} %convolution_add_fusion.5), channel_id=1, source_target_pairs={{0,4},{4,8},{8,12},{12,16},{16,20},{20,24},{24,28},{1,5},{5,9},{9,... | collective-permute-start | bytes 786440 | tf_op jit(solution)/shard_map/while/body/eval_jaxpr/ppermute | solution.py:14
  719.8 4.2 copy-start.11
  724.0 4.2 copy-start.19
  728.2 4.2 copy-start.7
  732.3 4.5 copy-start.5
  752.0 5.6 copy-start.1
Sparse Core Ops, SparseCore 0:
  8.9 17.6 all-gather.5
  28.8 147.9 all-gather.3
  178.8 124.7 all-gather.7
where the time goes:
time: 777 us; the launch traced here: 765 us
  other arithmetic  343 us (44%)
  waiting for transfers between devices  192 us (25%)
  local copies, waits for them, and re-layouts  93 us (12%)
  matrix products  70.3 us (9%)
  blocking collectives  42.1 us (5%)
  between operations  14.2 us (2%)
  starting transfers between devices  9.12 us (1%)
    another operation x2, other arithmetic, shards(): lax.linalg.triangular_solve(system, (beta_steps * jnp.exp(running))[...,...  316 us
    all_gather x1, waiting for transfers between devices, shards(): lax.all_gather(w_proj, 'ctx', axis=0, tiled=True)  134 us
    ppermute x7, waiting for transfers between devices, from_behind(): return lax.ppermute(array, axis, pairs)  57 us
    pad x7, local copies, waits for them, and re-layouts, shards(): inclusive = lax.associative_scan(compose, (transitions, writes), axis=1)  41.8 us
    all_gather x1, blocking collectives, shards(): lax.all_gather(w_small, 'ctx', axis=0, tiled=True)  30.7 us
    unnamed x47, local copies, waits for them, and re-layouts  18.6 us
    transpose x5, local copies, waits for them, and re-layouts, to_steps(): moved = jnp.moveaxis(array, 1, 0)  18 us
  transfers between devices with their start and end apart: 10, of which 8 were waited for; matrix products, arithmetic and copies ran while one was open for 65% of the time, Pallas kernels for 0%

commit v1 on v0

v1 whole, which is shorter than its diff:
```python
import functools
import math

import jax
import jax.numpy as jnp
from jax import lax
from jax.experimental import pallas as pl
from jax.experimental.pallas import tpu as pltpu
from jax.sharding import PartitionSpec as P

F32 = jnp.float32
BF16 = jnp.bfloat16
NN = (((1,), (0,)), ((), ()))
NT = (((1,), (1,)), ((), ()))
TN = (((0,), (0,)), ((), ()))
BLOCK = 64
BASE = 8


def dot1(left, right, dims=NN):
    return lax.dot_general(left, right, dims, preferred_element_type=F32)


def halves(array):
    high = array.astype(BF16)
    return high, (array - high.astype(F32)).astype(BF16)


def dot3(left, right, dims=NN):
    left_high, left_low = halves(left)
    right_high, right_low = halves(right)
    return (
        dot1(left_high, right_high, dims)
        + dot1(left_high, right_low, dims)
        + dot1(left_low, right_high, dims)
    )


def unit(vectors):
    return vectors * lax.rsqrt(jnp.sum(vectors * vectors, axis=-1, keepdims=True) + 1e-06)


def chunk_kernel(heads, mirrors, width, proj_ref, gate_ref, bias_ref, rate_ref, pre_ref, reach_ref, total_ref):
    toks = proj_ref.shape[0]
    span = toks * mirrors
    parts = 1 + 2 * mirrors
    gates = mirrors + 1

    @pl.when(pl.program_id(0) == 0)
    def _():
        rows = lax.broadcasted_iota(jnp.int32, (2 * width, width), 0)
        cols = lax.broadcasted_iota(jnp.int32, (2 * width, width), 1)
        start = jnp.where(rows == cols, 1.0, 0.0).astype(F32)
        for head in range(heads):
            total_ref[head] = start

    gate = gate_ref[...]
    strength = 2.0 / (1.0 + jnp.exp(-(gate + bias_ref[...])))
    log_decay = -rate_ref[...] * (jnp.maximum(gate, 0.0) + jnp.log(1.0 + jnp.exp(-jnp.abs(gate))))
    tok_r = lax.broadcasted_iota(jnp.int32, (toks, toks), 0)
    tok_c = lax.broadcasted_iota(jnp.int32, (toks, toks), 1)
    upto = jnp.where(tok_r >= tok_c, 1.0, 0.0).astype(F32)
    summed = lax.dot_general(
        upto, log_decay, NN, precision=lax.Precision.HIGHEST, preferred_element_type=F32
    )
    step_r = lax.broadcasted_iota(jnp.int32, (span, span), 0)
    step_c = lax.broadcasted_iota(jnp.int32, (span, span), 1)
    place_r = (step_r % toks) * mirrors + step_r // toks
    place_c = (step_c % toks) * mirrors + step_c // toks
    strict = place_r > place_c
    diagonal = step_r == step_c
    eye = jnp.where(diagonal, 1.0, 0.0).astype(F32)
    see_r = lax.broadcasted_iota(jnp.int32, (toks, span), 0)
    see_c = lax.broadcasted_iota(jnp.int32, (toks, span), 1)
    visible = see_c % toks <= see_r

    each = range(heads)

    def part(head, index):
        at = (head * parts + index) * width
        return proj_ref[:, at : at + width]

    query = [unit(part(h, 0)) for h in each]
    keys = [jnp.concatenate([unit(part(h, 1 + r)) for r in range(mirrors)], axis=0) for h in each]
    values = [jnp.concatenate([part(h, 1 + mirrors + r) for r in range(mirrors)], axis=0) for h in each]
    beta = [
        jnp.concatenate([strength[:, h * gates + r : h * gates + r + 1] for r in range(mirrors)], axis=0)
        for h in each
    ]
    run_q = [summed[:, h * gates + mirrors : h * gates + mirrors + 1] for h in each]
    run = [jnp.concatenate([run_q[h]] * mirrors, axis=0) for h in each]
    run_row = [jnp.sum(jnp.where(diagonal, run[h], 0.0), axis=0, keepdims=True) for h in each]
    last = [run_q[h][toks - 1 :, :] for h in each]
    inner = [dot3(jnp.concatenate([keys[h], query[h]], axis=0), keys[h], NT) for h in each]
    lower = [
        jnp.where(strict, beta[h] * jnp.exp(jnp.where(strict, run[h] - run_row[h], 0.0)) * inner[h][:span], 0.0)
        for h in each
    ]
    attend = [
        jnp.where(visible, jnp.exp(jnp.where(visible, run_q[h] - run_row[h], 0.0)) * inner[h][span:], 0.0)
        for h in each
    ]
    low_high = [halves(lower[h]) for h in each]
    near = place_r // BASE == place_c // BASE
    zero = jnp.zeros((), BF16)
    power = [jnp.where(near, low_high[h][0], zero) for h in each]
    inv = [eye - jnp.where(near, lower[h], 0.0) for h in each]
    reached = 2
    while reached < BASE:
        power = [dot1(power[h], power[h]).astype(BF16) for h in each]
        inv = [inv[h] + dot1(inv[h].astype(BF16), power[h]) for h in each]
        reached *= 2
    size = BASE
    while size < span:
        joined = (place_r // (2 * size) == place_c // (2 * size)) & (place_r // size != place_c // size)
        inv_now = [inv[h].astype(BF16) for h in each]
        cross = [dot1(jnp.where(joined, low_high[h][0], zero), inv_now[h]).astype(BF16) for h in each]
        inv = [inv[h] - dot1(inv_now[h], cross[h]) for h in each]
        size *= 2
    rough = [inv[h].astype(BF16) for h in each]
    left = [
        (eye - rough[h].astype(F32)) - dot1(low_high[h][0], rough[h]) - dot1(low_high[h][1], rough[h])
        for h in each
    ]
    inv = [rough[h].astype(F32) + dot1(rough[h], left[h].astype(BF16)) for h in each]

    given = [
        jnp.concatenate([beta[h] * values[h], (beta[h] * jnp.exp(run[h])) * keys[h]], axis=1) for h in each
    ]
    weighted = [dot3(inv[h], given[h]) for h in each]
    tails = [jnp.exp(last[h] - run[h]) * keys[h] for h in each]
    moved = [dot3(weighted[h], tails[h], TN) for h in each]
    seen = [dot3(attend[h], weighted[h]) for h in each]
    asked = [jnp.exp(run_q[h]) * query[h] - seen[h][:, width:] for h in each]
    before = [total_ref[h] for h in each]
    answers = [dot3(asked[h], before[h], NT) for h in each]
    after = [dot3(before[h], moved[h][width:]) for h in each]
    for h in each:
        reach_ref[:, h * width : (h + 1) * width] = answers[h][:, :width]
        pre_ref[:, h * width : (h + 1) * width] = answers[h][:, width:] + seen[h][:, :width]
        carried = jnp.exp(last[h]) * before[h] - after[h]
        total_ref[h, :width] = carried[:width]
        total_ref[h, width:] = carried[width:] + moved[h][:width]


def chunk_call(projected, gate_inputs, bias_row, rate_row, heads, mirrors, width, interpret=False):
    toks = projected.shape[0]
    block = math.gcd(toks, BLOCK)
    gates = gate_inputs.shape[1]
    span = block * mirrors
    units = toks // block * heads
    return pl.pallas_call(
        functools.partial(chunk_kernel, heads, mirrors, width),
        grid=(toks // block,),
        in_specs=[
            pl.BlockSpec((block, projected.shape[1]), lambda i: (i, 0)),
            pl.BlockSpec((block, gates), lambda i: (i, 0)),
            pl.BlockSpec((1, gates), lambda i: (0, 0)),
            pl.BlockSpec((1, gates), lambda i: (0, 0)),
        ],
        out_specs=[
            pl.BlockSpec((block, heads * width), lambda i: (i, 0)),
            pl.BlockSpec((block, heads * width), lambda i: (i, 0)),
            pl.BlockSpec((heads, 2 * width, width), lambda i: (0, 0, 0)),
        ],
        out_shape=[
            jax.ShapeDtypeStruct((toks, heads * width), F32),
            jax.ShapeDtypeStruct((toks, heads * width), F32),
            jax.ShapeDtypeStruct((heads, 2 * width, width), F32),
        ],
        compiler_params=pltpu.CompilerParams(vmem_limit_bytes=48 * 2**20),
        cost_estimate=pl.CostEstimate(
            flops=2 * units * 60 * span * span * width, bytes_accessed=4 * projected.size, transcendentals=0
        ),
        interpret=interpret,
    )(projected, gate_inputs, bias_row, rate_row)


def finish_kernel(heads, width, pre_ref, reach_ref, state_ref, out_ref):
    for head in range(heads):
        cols = slice(head * width, (head + 1) * width)
        out = pre_ref[:, cols] + dot3(reach_ref[:, cols], state_ref[head], NT)
        scale = lax.rsqrt(jnp.mean(out * out, axis=-1, keepdims=True) + 1e-06)
        out_ref[:, cols] = (out * scale).astype(BF16)


def finish_call(pre, reach, state, heads, width, interpret=False):
    return pl.pallas_call(
        functools.partial(finish_kernel, heads, width),
        out_shape=jax.ShapeDtypeStruct(pre.shape, BF16),
        compiler_params=pltpu.CompilerParams(vmem_limit_bytes=32 * 2**20),
        cost_estimate=pl.CostEstimate(
            flops=6 * pre.size * width, bytes_accessed=10 * pre.size, transcendentals=0
        ),
        interpret=interpret,
    )(pre, reach, state)


def from_behind(array, axis, by):
    count = lax.axis_size(axis)
    pairs = [(i, i + by) for i in range(count) if 0 <= i + by < count]
    return lax.ppermute(array, axis, pairs)


def matrix_product(left, right):
    return jnp.matmul(left, right, precision=lax.Precision.HIGHEST)


def gate_rows(beta_bias, decay_rate):
    heads, mirrors = beta_bias.shape
    bias = jnp.concatenate([beta_bias, jnp.zeros((heads, 1), F32)], axis=1).reshape(1, -1)
    rate = jnp.concatenate([jnp.zeros((heads, mirrors), F32), decay_rate[:, None]], axis=1).reshape(1, -1)
    return bias, rate


def shards(tokens, w_proj, w_small, beta_bias, decay_rate, w_out):
    tok_rows = tokens.shape[0]
    heads_here, mirrors = beta_bias.shape
    head_width = w_proj.shape[1] // (heads_here * (1 + 2 * mirrors))
    wide = w_proj.shape[1]
    fill = -w_small.shape[1] % 128
    both = jnp.concatenate([w_proj, jnp.pad(w_small, ((0, 0), (0, fill)))], axis=1)
    both = lax.all_gather(both, "ctx", axis=0, tiled=True)
    projected = jnp.dot(tokens, both, preferred_element_type=F32)
    later_out, projected = lax.optimization_barrier((w_out, projected))
    gate_inputs = projected[:, wide : wide + w_small.shape[1]]
    projected = projected[:, :wide]
    bias_row, rate_row = gate_rows(beta_bias, decay_rate)
    pre, reach, total = chunk_call(
        projected, gate_inputs, bias_row, rate_row, heads_here, mirrors, head_width
    )
    device_trans = total[:, :head_width]
    device_write = total[:, head_width:]

    def relay(turn, incoming):
        outgoing = matrix_product(incoming, device_trans) + device_write
        return from_behind(outgoing, "ctx", 1)

    state_in = lax.fori_loop(
        0, lax.axis_size("ctx") - 1, relay, jnp.zeros(device_write.shape, F32)
    )
    mixed_heads = finish_call(pre, reach, state_in, heads_here, head_width)
    grouped = lax.all_gather(later_out, "head", axis=0, tiled=True)
    full_out = lax.all_gather(grouped, "ctx", axis=1, tiled=True)
    group_count = lax.axis_size("head")
    rows_each = tok_rows // group_count
    stacked = mixed_heads.reshape(group_count, rows_each, heads_here * head_width)
    mixed = jnp.einsum(
        "irk,kd->ird",
        lax.all_to_all(stacked, "head", split_axis=0, concat_axis=2, tiled=True),
        full_out,
        preferred_element_type=F32,
    ).astype(BF16)
    return mixed.reshape(rows_each, full_out.shape[1])


def solution(mesh):
    placed = (
        P("ctx", None),
        P("ctx", "head"),
        P("ctx", "head"),
        P("head", None),
        P("head"),
        P("head", "ctx"),
    )
    return jax.shard_map(
        shards, mesh=mesh, in_specs=placed, out_specs=P(("ctx", "head"), None), check_vma=False
    )
```

time: 777 us -> 389 us (0.50); the launches traced: 765 us -> 385 us
  other arithmetic: 343 us -> 2.51 us
  waiting for transfers between devices: 192 us -> 285 us
  local copies, waits for them, and re-layouts: 93 us -> 12.2 us
  matrix products: 70.3 us -> 20.1 us
  Pallas kernels: 0 us -> 31.4 us
  blocking collectives: 42.1 us -> 11.2 us
    another operation x3 -> x0, other arithmetic: 317 us -> none  [the longest x2 316 us: shards(): lax.linalg.triangular_solve(system, (beta_steps * jnp.exp(running))[...,...]
    ppermute x7, waiting for transfers between devices: 57 us -> 112 us  [from_behind(): return lax.ppermute(array, axis, pairs)]
    pad x7 -> x0, local copies, waits for them, and re-layouts: 41.8 us -> none  [shards(): inclusive = lax.associative_scan(compose, (transitions, writes), axis=1)]
    dot_general x27 -> x8, matrix products: 55.4 us -> 14.7 us  [the longest x1 11.9 us: shards(): projected = jnp.dot(tokens, both, preferred_element_type=F32)]
    all_gather x2, waiting for transfers between devices: 134 us -> 173 us  [the longest x1 155 us: shards(): both = lax.all_gather(both, 'ctx', axis=0, tiled=True)]
    pallas_call x0 -> x2, Pallas kernels: none -> 31.4 us  [the longest x1 30.7 us: chunk_call(): pl.pallas_call(functools.partial(chunk_kernel, heads, mirrors, width), gr...]
    all_gather x1 -> x0, blocking collectives: 30.7 us -> none  [shards(): lax.all_gather(w_small, 'ctx', axis=0, tiled=True)]
    transpose x6 -> x0, local copies, waits for them, and re-layouts: 20.6 us -> none  [the longest x5 18 us: to_steps(): moved = jnp.moveaxis(array, 1, 0)]
  transfers between devices with their start and end apart: 10 -> 10, of which waited for: 8 -> 9; matrix products, arithmetic and copies ran while one was open for 65% -> 2% of each run, Pallas kernels for 0% -> 8%
where the time goes in v1:
time: 389 us; the launch traced here: 385 us
  waiting for transfers between devices  285 us (73%)
  Pallas kernels  31.4 us (8%)
  matrix products  20.1 us (5%)
  between operations  13.2 us (3%)
  local copies, waits for them, and re-layouts  12.2 us (3%)
  blocking collectives  11.2 us (3%)
  starting transfers between devices  9.13 us (2%)
    all_gather x1, waiting for transfers between devices, shards(): both = lax.all_gather(both, 'ctx', axis=0, tiled=True)  155 us
    ppermute x7, waiting for transfers between devices, from_behind(): return lax.ppermute(array, axis, pairs)  112 us
    pallas_call x1, Pallas kernels, chunk_call(): pl.pallas_call(functools.partial(chunk_kernel, heads, mirrors, width), gr...  30.7 us
    all_gather x1, waiting for transfers between devices, shards(): grouped = lax.all_gather(later_out, 'head', axis=0, tiled=True)  17.9 us
    dot_general x1, matrix products, shards(): projected = jnp.dot(tokens, both, preferred_element_type=F32)  11.9 us
    all_to_all x1, blocking collectives, shards(): lax.all_to_all(stacked, 'head', split_axis=0, concat_axis=2, tiled=True)  11.2 us
    ppermute x7, starting transfers between devices, from_behind(): return lax.ppermute(array, axis, pairs)  9.04 us
  transfers between devices with their start and end apart: 10, of which 9 were waited for; matrix products, arithmetic and copies ran while one was open for 2% of the time, Pallas kernels for 8%

profile of v1, /device:TPU:28, one launch (start us, length us, event | category | flops | bytes accessed | tf_op | source)
XLA Modules:
  0.0 385.2 jit_solution(12658455100845734725)
XLA Ops:
  6.5 0.0 copy-start
  6.5 0.0 all-gather.4.cloned.1.call-start
  6.5 1.0 copy.17
  7.5 2.5 fusion.1
  10.0 0.0 all-gather.4.cloned.1.call-update
  10.1 0.0 copy-start.5
  10.1 0.0 copy-start.6
  10.1 0.0 all-gather.6.cloned.1.call-start
  10.1 155.3 %all-gather.4.cloned.1.call-done = bf16[2048,2688]{1,0:T(8,128)(2,1)} async-done(((bf16[256,2688]{1,0:T(8,128)(2,1)}), bf16[2048,2688]{1,0:T(8,128)(2,1)}) %all-gather.4.cloned.1.call-update) | async-done | bytes 11010064 | tf_op jit(solution)/shard_map/all_gather | solution.py:223
  165.5 0.0 copy-done
  165.5 11.9 %convolution_bitcast_fusion = f32[512,2688]{1,0:T(8,128)} fusion(bf16[512,2048]{1,0:T(8,128)(2,1)S(1)} %copy-done, bf16[2048,2688]{1,0:T(8,128)(2,1)} %all-gather.4.cloned.1.call-done), kind=kOutput, calls=%fused_computation.1 | convolution fusion | flops 5637144576 | bytes 18612224 | tf_op jit(solution)/shard_map/dot_general | solution.py:224
  177.4 0.0 all-gather.6.cloned.1.call-update
  177.4 0.0 all-gather.8.cloned.1.call-start
  177.5 17.9 %all-gather.6.cloned.1.call-done = bf16[2048,256]{1,0:T(8,128)(2,1)} async-done(((bf16[512,256]{1,0:T(8,128)(2,1)}), bf16[2048,256]{1,0:T(8,128)(2,1)}) %all-gather.6.cloned.1.call-update) | async-done | bytes 1048592 | tf_op jit(solution)/shard_map/all_gather | solution.py:243
  195.4 0.0 all-gather.8.cloned.1.call-update
  195.4 0.0 copy-done.5
  195.5 0.1 copy.18
  195.6 0.1 reshape.17.bias_ref
  195.6 0.0 copy-done.6
  195.6 0.1 copy.19
  195.7 0.1 concatenate.11.clone
  195.8 0.1 reshape.18.rate_ref
  195.9 5.1 %slice.12.proj_ref = f32[512,2560]{1,0:T(8,128)} slice(f32[512,2688]{1,0:T(8,128)} %convolution_bitcast_fusion), slice={[0:512], [0:2560]} | slice | bytes 10485760 | tf_op jit(solution)/shard_map/slice | solution.py:227
  201.0 1.0 slice.13.gate_ref
  202.0 30.7 %shard_map.64 = (f32[512,512]{1,0:T(8,128)S(1)}, f32[512,512]{1,0:T(8,128)S(1)}, f32[4,256,128]{2,1,0:T(8,128)S(1)}) custom-call(f32[512,2560]{1,0:T(8,128)} %slice.12.proj_ref, f32[512,12]{1,0:T(8,128)S(1)} %slice.13.gate_ref, f32[1,12]{1,0:T(1,128)S(1)} %reshape.17.bias_ref, f32[1,12]{1,0:T(1,128)S(1)} %reshape.18.rate_ref), custom_call_target="tpu_custom_call" | custom-call | flops 8053063680 | bytes 5242880 | tf_op jit(solution)/shard_map/pallas_call | solution.py:152
  232.7 0.0 copy-start.1
  232.7 1.0 copy-done.1
  233.7 0.0 copy-start.3
  233.7 1.0 copy-done.3
  234.7 123.8 %while.10 = (s32[]{:T(128)}, f32[4,128,128]{2,1,0:T(8,128)S(1)}, f32[4,128,128]{2,1,0:T(8,128)S(1)}, f32[4,128,128]{2,1,0:T(8,128)S(1)}, s32[]{:T(128)}) while((s32[]{:T(128)}, f32[4,128,128]{2,1,0:T(8,128)S(1)}, f32[4,128,128]{2,1,0:T(8,128)S(1)}, f32[4,128,128]{2,1,0:T(8,128)S(1)}, s32[]{:T(128)}) %tuple.21), condition=%wide.region_1.2_spmd, body=%wide.region_0.1_spmd.sunk | while | flops 100728832 | bytes 2097253 | solution.py:239
  234.7 0.4 convolution_add_fusion.2
  235.1 1.3 collective-permute-start
  236.4 9.0 %collective-permute-done = f32[4,128,128]{2,1,0:T(8,128)S(1)} collective-permute-done((f32[4,128,128]{2,1,0:T(8,128)S(1)}, f32[4,128,128]{2,1,0:T(8,128)S(1)}, u32[]{:S(2)}, u32[]{:S(2)}) %collective-permute-start) | collective-permute-done | bytes 262176 | tf_op jit(solution)/shard_map/while/body/eval_jaxpr/ppermute | solution.py:202
  245.5 0.4 convolution_add_fusion.2
  245.9 1.3 collective-permute-start
  247.2 16.5 %collective-permute-done = f32[4,128,128]{2,1,0:T(8,128)S(1)} collective-permute-done((f32[4,128,128]{2,1,0:T(8,128)S(1)}, f32[4,128,128]{2,1,0:T(8,128)S(1)}, u32[]{:S(2)}, u32[]{:S(2)}) %collective-permute-start) | collective-permute-done | bytes 262176 | tf_op jit(solution)/shard_map/while/body/eval_jaxpr/ppermute | solution.py:202
  263.7 0.4 convolution_add_fusion.2
  264.1 1.3 collective-permute-start
  265.4 19.0 %collective-permute-done = f32[4,128,128]{2,1,0:T(8,128)S(1)} collective-permute-done((f32[4,128,128]{2,1,0:T(8,128)S(1)}, f32[4,128,128]{2,1,0:T(8,128)S(1)}, u32[]{:S(2)}, u32[]{:S(2)}) %collective-permute-start) | collective-permute-done | bytes 262176 | tf_op jit(solution)/shard_map/while/body/eval_jaxpr/ppermute | solution.py:202
  284.4 0.4 convolution_add_fusion.2
  284.8 1.3 collective-permute-start
  286.1 22.6 %collective-permute-done = f32[4,128,128]{2,1,0:T(8,128)S(1)} collective-permute-done((f32[4,128,128]{2,1,0:T(8,128)S(1)}, f32[4,128,128]{2,1,0:T(8,128)S(1)}, u32[]{:S(2)}, u32[]{:S(2)}) %collective-permute-start) | collective-permute-done | bytes 262176 | tf_op jit(solution)/shard_map/while/body/eval_jaxpr/ppermute | solution.py:202
  308.8 0.4 convolution_add_fusion.2
  309.2 1.3 collective-permute-start
  310.5 13.8 %collective-permute-done = f32[4,128,128]{2,1,0:T(8,128)S(1)} collective-permute-done((f32[4,128,128]{2,1,0:T(8,128)S(1)}, f32[4,128,128]{2,1,0:T(8,128)S(1)}, u32[]{:S(2)}, u32[]{:S(2)}) %collective-permute-start) | collective-permute-done | bytes 262176 | tf_op jit(solution)/shard_map/while/body/eval_jaxpr/ppermute | solution.py:202
  324.2 0.4 convolution_add_fusion.2
  324.6 1.3 collective-permute-start
  325.9 16.2 %collective-permute-done = f32[4,128,128]{2,1,0:T(8,128)S(1)} collective-permute-done((f32[4,128,128]{2,1,0:T(8,128)S(1)}, f32[4,128,128]{2,1,0:T(8,128)S(1)}, u32[]{:S(2)}, u32[]{:S(2)}) %collective-permute-start) | collective-permute-done | bytes 262176 | tf_op jit(solution)/shard_map/while/body/eval_jaxpr/ppermute | solution.py:202
  342.1 0.4 convolution_add_fusion.2
  342.5 1.3 collective-permute-start
  343.8 14.7 %collective-permute-done = f32[4,128,128]{2,1,0:T(8,128)S(1)} collective-permute-done((f32[4,128,128]{2,1,0:T(8,128)S(1)}, f32[4,128,128]{2,1,0:T(8,128)S(1)}, u32[]{:S(2)}, u32[]{:S(2)}) %collective-permute-start) | collective-permute-done | bytes 262176 | tf_op jit(solution)/shard_map/while/body/eval_jaxpr/ppermute | solution.py:202
  358.5 0.0 copy-start.2
  358.5 1.2 copy-done.2
  359.8 0.0 copy-start.4
  359.8 1.2 copy-done.4
  361.0 0.7 shard_map.65
  361.7 0.3 copy.15
  362.0 11.2 %all_to_all.15 = bf16[4,128,512]{1,2,0:T(8,128)(2,1)S(1)} all-to-all(bf16[4,128,512]{1,2,0:T(8,128)(2,1)S(1)} %copy.15), channel_id=1, replica_groups=mesh['ctx'=8,'head'=4] {'head'}, dimensions={0} | all-to-all | bytes 1048576 | tf_op jit(solution)/shard_map/all_to_all | solution.py:250
  373.3 0.0 all-gather.8.cloned.1.call-done
  373.3 5.5 %convolution_convert_fusion = bf16[128,2048]{1,0:T(8,128)(2,1)} fusion(bf16[128,2048]{0,1:T(8,128)(2,1)S(1)} %bitcast.20, bf16[2048,2048]{1,0:T(8,128)(2,1)} %all-gather.8.cloned.1.call-done), kind=kOutput, calls=%fused_computation.4 | convolution fusion | flops 1074003968 | bytes 9437184 | tf_op jit(solution)/shard_map/irk,kd->ird/dot_general | solution.py:248
  (3 shorter events, 0.1 us)
Async XLA Ops:
  6.5 158.9 %copy-start = (bf16[512,2048]{1,0:T(8,128)(2,1)S(1)}, bf16[512,2048]{1,0:T(8,128)(2,1)}, u32[]{:S(2)}) copy-start(bf16[512,2048]{1,0:T(8,128)(2,1)} %param.8) | copy-start | bytes 6291460
  6.5 158.9 %all-gather.4.cloned.1.call-start = ((), (), s32[]{:S(2)}) async-start(), calls=%async_computation.1 | async-start | bytes 12386304 | tf_op jit(solution)/shard_map/all_gather | solution.py:223
  10.1 185.4 %copy-start.5 = (f32[4,2]{0,1:T(2,128)S(1)}, f32[4,2]{0,1:T(2,128)}, u32[]{:S(2)}) copy-start(f32[4,2]{0,1:T(2,128)} %param.11) | copy-start | bytes 100
  10.1 185.6 %copy-start.6 = (f32[4]{0:T(128)S(1)}, f32[4]{0:T(128)}, u32[]{:S(2)}) copy-start(f32[4]{0:T(128)} %param.12) | copy-start | bytes 52
  10.1 185.3 %all-gather.6.cloned.1.call-start = ((), (), s32[]{:S(2)}) async-start(), calls=%async_computation.2 | async-start | bytes 1310720 | tf_op jit(solution)/shard_map/all_gather | solution.py:243
  177.4 195.8 %all-gather.8.cloned.1.call-start = ((), (), s32[]{:S(2)}) async-start(), calls=%async_computation.3 | async-start | bytes 9437184 | tf_op jit(solution)/shard_map/all_gather | solution.py:244
  232.7 1.0 copy-start.1
  233.7 1.0 copy-start.3
  235.1 10.3 %collective-permute-start = (f32[4,128,128]{2,1,0:T(8,128)S(1)}, f32[4,128,128]{2,1,0:T(8,128)S(1)}, u32[]{:S(2)}, u32[]{:S(2)}) collective-permute-start(f32[4,128,128]{2,1,0:T(8,128)S(1)} %convolution_add_fusion.2), channel_id=1, source_target_pairs={{0,4},{4,8},{8,12},{12,16},{16,20},{20,24},{24,28},{1,5},{5,9},{9,... | collective-permute-start | bytes 786440 | tf_op jit(solution)/shard_map/while/body/eval_jaxpr/ppermute | solution.py:202
  245.9 17.8 %collective-permute-start = (f32[4,128,128]{2,1,0:T(8,128)S(1)}, f32[4,128,128]{2,1,0:T(8,128)S(1)}, u32[]{:S(2)}, u32[]{:S(2)}) collective-permute-start(f32[4,128,128]{2,1,0:T(8,128)S(1)} %convolution_add_fusion.2), channel_id=1, source_target_pairs={{0,4},{4,8},{8,12},{12,16},{16,20},{20,24},{24,28},{1,5},{5,9},{9,... | collective-permute-start | bytes 786440 | tf_op jit(solution)/shard_map/while/body/eval_jaxpr/ppermute | solution.py:202
  264.1 20.3 %collective-permute-start = (f32[4,128,128]{2,1,0:T(8,128)S(1)}, f32[4,128,128]{2,1,0:T(8,128)S(1)}, u32[]{:S(2)}, u32[]{:S(2)}) collective-permute-start(f32[4,128,128]{2,1,0:T(8,128)S(1)} %convolution_add_fusion.2), channel_id=1, source_target_pairs={{0,4},{4,8},{8,12},{12,16},{16,20},{20,24},{24,28},{1,5},{5,9},{9,... | collective-permute-start | bytes 786440 | tf_op jit(solution)/shard_map/while/body/eval_jaxpr/ppermute | solution.py:202
  284.8 23.9 %collective-permute-start = (f32[4,128,128]{2,1,0:T(8,128)S(1)}, f32[4,128,128]{2,1,0:T(8,128)S(1)}, u32[]{:S(2)}, u32[]{:S(2)}) collective-permute-start(f32[4,128,128]{2,1,0:T(8,128)S(1)} %convolution_add_fusion.2), channel_id=1, source_target_pairs={{0,4},{4,8},{8,12},{12,16},{16,20},{20,24},{24,28},{1,5},{5,9},{9,... | collective-permute-start | bytes 786440 | tf_op jit(solution)/shard_map/while/body/eval_jaxpr/ppermute | solution.py:202
  309.2 15.1 %collective-permute-start = (f32[4,128,128]{2,1,0:T(8,128)S(1)}, f32[4,128,128]{2,1,0:T(8,128)S(1)}, u32[]{:S(2)}, u32[]{:S(2)}) collective-permute-start(f32[4,128,128]{2,1,0:T(8,128)S(1)} %convolution_add_fusion.2), channel_id=1, source_target_pairs={{0,4},{4,8},{8,12},{12,16},{16,20},{20,24},{24,28},{1,5},{5,9},{9,... | collective-permute-start | bytes 786440 | tf_op jit(solution)/shard_map/while/body/eval_jaxpr/ppermute | solution.py:202
  324.6 17.5 %collective-permute-start = (f32[4,128,128]{2,1,0:T(8,128)S(1)}, f32[4,128,128]{2,1,0:T(8,128)S(1)}, u32[]{:S(2)}, u32[]{:S(2)}) collective-permute-start(f32[4,128,128]{2,1,0:T(8,128)S(1)} %convolution_add_fusion.2), channel_id=1, source_target_pairs={{0,4},{4,8},{8,12},{12,16},{16,20},{20,24},{24,28},{1,5},{5,9},{9,... | collective-permute-start | bytes 786440 | tf_op jit(solution)/shard_map/while/body/eval_jaxpr/ppermute | solution.py:202
  342.5 16.0 %collective-permute-start = (f32[4,128,128]{2,1,0:T(8,128)S(1)}, f32[4,128,128]{2,1,0:T(8,128)S(1)}, u32[]{:S(2)}, u32[]{:S(2)}) collective-permute-start(f32[4,128,128]{2,1,0:T(8,128)S(1)} %convolution_add_fusion.2), channel_id=1, source_target_pairs={{0,4},{4,8},{8,12},{12,16},{16,20},{20,24},{24,28},{1,5},{5,9},{9,... | collective-permute-start | bytes 786440 | tf_op jit(solution)/shard_map/while/body/eval_jaxpr/ppermute | solution.py:202
  358.5 1.2 copy-start.2
  359.8 1.2 copy-start.4
Sparse Core Ops, SparseCore 0:
  10.2 155.2 all-gather.3
  177.5 17.8 all-gather.5
  197.5 153.4 all-gather.7

commit v2 on v1

--- a/solution.py
+++ b/solution.py
@@ -176,34 +176,93 @@
     )(projected, gate_inputs, bias_row, rate_row)
 
 
-def finish_kernel(heads, width, pre_ref, reach_ref, state_ref, out_ref):
+def relay_kernel(heads, width, pre_ref, reach_ref, total_ref, out_ref, inbox, outbox, send_sem, recv_sem):
+    me = lax.axis_index("ctx")
+    group = lax.axis_index("head")
+    count = lax.axis_size("ctx")
+    first = me == 0
+    final = me == count - 1
+    barrier = pltpu.get_barrier_semaphore()
+
+    def greet(other):
+        pl.semaphore_signal(barrier, inc=1, device_id=(other, group), device_id_type=pl.DeviceIdType.MESH)
+
+    @pl.when(jnp.logical_not(first))
+    def _():
+        greet(me - 1)
+
+    @pl.when(jnp.logical_not(final))
+    def _():
+        greet(me + 1)
+
+    edge = jnp.logical_or(first, final)
+
+    @pl.when(edge)
+    def _():
+        pl.semaphore_wait(barrier, 1)
+
+    @pl.when(jnp.logical_not(edge))
+    def _():
+        pl.semaphore_wait(barrier, 2)
+
+    def copy(head):
+        return pltpu.make_async_remote_copy(
+            src_ref=outbox.at[head],
+            dst_ref=inbox.at[head],
+            send_sem=send_sem.at[head],
+            recv_sem=recv_sem.at[head],
+            device_id=(lax.rem(me + 1, count), group),
+            device_id_type=pl.DeviceIdType.MESH,
+        )
+
+    @pl.when(first)
+    def _():
+        for head in range(heads):
+            inbox[head] = jnp.zeros((width, width), F32)
+            outbox[head] = total_ref[head, width:]
+            copy(head).start()
+
+    @pl.when(jnp.logical_not(first))
+    def _():
+        for head in range(heads):
+            copy(head).wait_recv()
+
+            @pl.when(jnp.logical_not(final))
+            def _():
+                outbox[head] = dot3(inbox[head], total_ref[head, :width]) + total_ref[head, width:]
+                copy(head).start()
+
     for head in range(heads):
         cols = slice(head * width, (head + 1) * width)
-        out = pre_ref[:, cols] + dot3(reach_ref[:, cols], state_ref[head], NT)
+        out = pre_ref[:, cols] + dot3(reach_ref[:, cols], inbox[head], NT)
         scale = lax.rsqrt(jnp.mean(out * out, axis=-1, keepdims=True) + 1e-06)
         out_ref[:, cols] = (out * scale).astype(BF16)
 
-
-def finish_call(pre, reach, state, heads, width, interpret=False):
+    @pl.when(jnp.logical_not(final))
+    def _():
+        for head in range(heads):
+            copy(head).wait_send()
+
+
+def relay_call(pre, reach, total, heads, width):
     return pl.pallas_call(
-        functools.partial(finish_kernel, heads, width),
+        functools.partial(relay_kernel, heads, width),
         out_shape=jax.ShapeDtypeStruct(pre.shape, BF16),
-        compiler_params=pltpu.CompilerParams(vmem_limit_bytes=32 * 2**20),
+        in_specs=[pl.BlockSpec(memory_space=pltpu.VMEM)] * 3,
+        out_specs=pl.BlockSpec(memory_space=pltpu.VMEM),
+        scratch_shapes=[
+            pltpu.VMEM((heads, width, width), F32),
+            pltpu.VMEM((heads, width, width), F32),
+            pltpu.SemaphoreType.DMA((heads,)),
+            pltpu.SemaphoreType.DMA((heads,)),
+        ],
+        compiler_params=pltpu.CompilerParams(
+            collective_id=0, has_side_effects=True, vmem_limit_bytes=32 * 2**20
+        ),
         cost_estimate=pl.CostEstimate(
             flops=6 * pre.size * width, bytes_accessed=10 * pre.size, transcendentals=0
         ),
-        interpret=interpret,
-    )(pre, reach, state)
-
-
-def from_behind(array, axis, by):
-    count = lax.axis_size(axis)
-    pairs = [(i, i + by) for i in range(count) if 0 <= i + by < count]
-    return lax.ppermute(array, axis, pairs)
-
-
-def matrix_product(left, right):
-    return jnp.matmul(left, right, precision=lax.Precision.HIGHEST)
+    )(pre, reach, total)
 
 
 def gate_rows(beta_bias, decay_rate):
@@ -222,25 +281,15 @@
     both = jnp.concatenate([w_proj, jnp.pad(w_small, ((0, 0), (0, fill)))], axis=1)
     both = lax.all_gather(both, "ctx", axis=0, tiled=True)
     projected = jnp.dot(tokens, both, preferred_element_type=F32)
-    later_out, projected = lax.optimization_barrier((w_out, projected))
+    grouped = lax.all_gather(w_out, "head", axis=0, tiled=True)
+    grouped, projected = lax.optimization_barrier((grouped, projected))
     gate_inputs = projected[:, wide : wide + w_small.shape[1]]
     projected = projected[:, :wide]
     bias_row, rate_row = gate_rows(beta_bias, decay_rate)
     pre, reach, total = chunk_call(
         projected, gate_inputs, bias_row, rate_row, heads_here, mirrors, head_width
     )
-    device_trans = total[:, :head_width]
-    device_write = total[:, head_width:]
-
-    def relay(turn, incoming):
-        outgoing = matrix_product(incoming, device_trans) + device_write
-        return from_behind(outgoing, "ctx", 1)
-
-    state_in = lax.fori_loop(
-        0, lax.axis_size("ctx") - 1, relay, jnp.zeros(device_write.shape, F32)
-    )
-    mixed_heads = finish_call(pre, reach, state_in, heads_here, head_width)
-    grouped = lax.all_gather(later_out, "head", axis=0, tiled=True)
+    mixed_heads = relay_call(pre, reach, total, heads_here, head_width)
     full_out = lax.all_gather(grouped, "ctx", axis=1, tiled=True)
     group_count = lax.axis_size("head")
     rows_each = tok_rows // group_count

time: 389 us -> 332 us (0.85)
  waiting for transfers between devices: 285 us -> 191 us
  Pallas kernels: 31.4 us -> 84.9 us
  starting transfers between devices: 9.13 us -> 0.08 us
  local copies, waits for them, and re-layouts: 12.2 us -> 7.81 us
    ppermute x7 -> x0, waiting for transfers between devices: 112 us -> none  [from_behind(): return lax.ppermute(array, axis, pairs)]
    pallas_call x1, Pallas kernels: 0.74 us -> 54.2 us  [relay_call(): pl.pallas_call(functools.partial(relay_kernel, heads, width), out_shape=j...]
    all_gather x1, waiting for transfers between devices: 0.01 us -> 28.7 us  [shards(): full_out = lax.all_gather(grouped, 'ctx', axis=1, tiled=True)]
    all_gather x1, waiting for transfers between devices: 17.9 us -> 7.46 us  [shards(): grouped = lax.all_gather(w_out, 'head', axis=0, tiled=True)]
    ppermute x7 -> x0, starting transfers between devices: 9.04 us -> none  [from_behind(): return lax.ppermute(array, axis, pairs)]
    unnamed x17 -> x9, local copies, waits for them, and re-layouts: 5.58 us -> 1.18 us
  transfers between devices with their start and end apart: 10 -> 3, of which waited for: 9 -> 3; matrix products, arithmetic and copies ran while one was open for 2% -> 6% of each run, Pallas kernels for 8% -> 26%
where the time goes in v2:
time: 332 us; the launch traced here: 329 us
  waiting for transfers between devices  191 us (58%)
  Pallas kernels  84.9 us (26%)
  matrix products  17.4 us (5%)
  between operations  13.2 us (4%)
  blocking collectives  11.4 us (3%)
  local copies, waits for them, and re-layouts  7.81 us (2%)
    all_gather x1, waiting for transfers between devices, shards(): both = lax.all_gather(both, 'ctx', axis=0, tiled=True)  155 us
    pallas_call x1, Pallas kernels, relay_call(): pl.pallas_call(functools.partial(relay_kernel, heads, width), out_shape=j...  54.2 us
    pallas_call x1, Pallas kernels, chunk_call(): pl.pallas_call(functools.partial(chunk_kernel, heads, mirrors, width), gr...  30.7 us
    all_gather x1, waiting for transfers between devices, shards(): full_out = lax.all_gather(grouped, 'ctx', axis=1, tiled=True)  28.7 us
    dot_general x1, matrix products, shards(): projected = jnp.dot(tokens, both, preferred_element_type=F32)  12 us
    all_to_all x1, blocking collectives, shards(): lax.all_to_all(stacked, 'head', split_axis=0, concat_axis=2, tiled=True)  11.4 us
    all_gather x1, waiting for transfers between devices, shards(): grouped = lax.all_gather(w_out, 'head', axis=0, tiled=True)  7.46 us
  transfers between devices with their start and end apart: 3, of which 3 were waited for; matrix products, arithmetic and copies ran while one was open for 6% of the time, Pallas kernels for 26%

profile of v2, /device:TPU:28, one launch (start us, length us, event | category | flops | bytes accessed | tf_op | source)
XLA Modules:
  0.0 328.8 jit_solution(10572934510012105339)
XLA Ops:
  6.5 0.0 copy-start
  6.5 0.0 all-gather.6.cloned.1.call-start
  6.5 1.0 copy.17
  7.5 2.5 fusion.1
  10.0 0.0 all-gather.6.cloned.1.call-update
  10.0 0.0 all-gather.4.cloned.1.call-start
  10.1 0.7 all-gather.4.cloned.1.call-update
  10.8 0.0 copy-start.1
  10.8 0.0 copy-start.2
  10.8 0.0 all-gather.8.cloned.1.call-start
  10.9 154.6 %all-gather.6.cloned.1.call-done = bf16[2048,2688]{1,0:T(8,128)(2,1)} async-done(((bf16[256,2688]{1,0:T(8,128)(2,1)}), bf16[2048,2688]{1,0:T(8,128)(2,1)}) %all-gather.6.cloned.1.call-update) | async-done | bytes 11010064 | tf_op jit(solution)/shard_map/all_gather | solution.py:282
  165.5 0.0 copy-done
  165.5 12.0 %convolution_bitcast_fusion = f32[512,2688]{1,0:T(8,128)} fusion(bf16[512,2048]{1,0:T(8,128)(2,1)S(1)} %copy-done, bf16[2048,2688]{1,0:T(8,128)(2,1)} %all-gather.6.cloned.1.call-done), kind=kOutput, calls=%fused_computation | convolution fusion | flops 5637144576 | bytes 18612224 | tf_op jit(solution)/shard_map/dot_general | solution.py:283
  177.4 7.5 %all-gather.4.cloned.1.call-done = bf16[2048,256]{1,0:T(8,128)(2,1)} async-done(((bf16[512,256]{1,0:T(8,128)(2,1)}), bf16[2048,256]{1,0:T(8,128)(2,1)}) %all-gather.4.cloned.1.call-update) | async-done | bytes 1048592 | tf_op jit(solution)/shard_map/all_gather | solution.py:284
  184.9 0.0 all-gather.8.cloned.1.call-update
  184.9 0.0 copy-done.1
  184.9 0.1 copy.18
  185.0 0.1 reshape.17.bias_ref
  185.1 0.0 copy-done.2
  185.1 0.1 copy.19
  185.2 0.1 concatenate.11.clone
  185.3 0.1 reshape.18.rate_ref
  185.4 5.1 %slice.6.proj_ref = f32[512,2560]{1,0:T(8,128)} slice(f32[512,2688]{1,0:T(8,128)} %convolution_bitcast_fusion), slice={[0:512], [0:2560]} | slice | bytes 10485760 | tf_op jit(solution)/shard_map/slice | solution.py:287
  190.5 1.0 slice.7.gate_ref
  191.5 30.7 %shard_map.64 = (f32[512,512]{1,0:T(8,128)S(1)}, f32[512,512]{1,0:T(8,128)S(1)}, f32[4,256,128]{2,1,0:T(8,128)S(1)}) custom-call(f32[512,2560]{1,0:T(8,128)} %slice.6.proj_ref, f32[512,12]{1,0:T(8,128)S(1)} %slice.7.gate_ref, f32[1,12]{1,0:T(1,128)S(1)} %reshape.17.bias_ref, f32[1,12]{1,0:T(1,128)S(1)} %reshape.18.rate_ref), custom_call_target="tpu_custom_call" | custom-call | flops 8053063680 | bytes 5242880 | tf_op jit(solution)/shard_map/pallas_call | solution.py:152
  222.2 54.2 %shard_map.65 = bf16[512,512]{1,0:T(8,128)(2,1)S(1)} custom-call(f32[512,512]{1,0:T(8,128)S(1)} %get-tuple-element.11.pre_ref, f32[512,512]{1,0:T(8,128)S(1)} %get-tuple-element.12.reach_ref, f32[4,256,128]{2,1,0:T(8,128)S(1)} %get-tuple-element.13.total_ref), custom_call_target="tpu_custom_call" | custom-call | flops 201326592 | bytes 2621440 | tf_op jit(solution)/shard_map/pallas_call | solution.py:248
  276.4 0.3 copy.15
  276.7 11.4 %all_to_all.15 = bf16[4,128,512]{1,2,0:T(8,128)(2,1)S(1)} all-to-all(bf16[4,128,512]{1,2,0:T(8,128)(2,1)S(1)} %copy.15), channel_id=1, replica_groups=mesh['ctx'=8,'head'=4] {'head'}, dimensions={0} | all-to-all | bytes 1048576 | tf_op jit(solution)/shard_map/all_to_all | solution.py:299
  288.1 28.7 %all-gather.8.cloned.1.call-done = bf16[2048,2048]{1,0:T(8,128)(2,1)} async-done(((bf16[2048,256]{1,0:T(8,128)(2,1)}), bf16[2048,2048]{1,0:T(8,128)(2,1)}) %all-gather.8.cloned.1.call-update) | async-done | bytes 8388624 | tf_op jit(solution)/shard_map/all_gather | solution.py:293
  316.8 5.5 %convolution_convert_fusion = bf16[128,2048]{1,0:T(8,128)(2,1)} fusion(bf16[128,2048]{0,1:T(8,128)(2,1)S(1)} %bitcast.14, bf16[2048,2048]{1,0:T(8,128)(2,1)} %all-gather.8.cloned.1.call-done), kind=kOutput, calls=%fused_computation.3 | convolution fusion | flops 1074003968 | bytes 9437184 | tf_op jit(solution)/shard_map/irk,kd->ird/dot_general | solution.py:297
  (1 shorter events, 0.0 us)
Async XLA Ops:
  6.5 158.9 %copy-start = (bf16[512,2048]{1,0:T(8,128)(2,1)S(1)}, bf16[512,2048]{1,0:T(8,128)(2,1)}, u32[]{:S(2)}) copy-start(bf16[512,2048]{1,0:T(8,128)(2,1)} %param.6) | copy-start | bytes 6291460
  6.5 158.9 %all-gather.6.cloned.1.call-start = ((), (), s32[]{:S(2)}) async-start(), calls=%async_computation.2 | async-start | bytes 12386304 | tf_op jit(solution)/shard_map/all_gather | solution.py:282
  10.0 174.8 %all-gather.4.cloned.1.call-start = ((), (), s32[]{:S(2)}) async-start(), calls=%async_computation.1 | async-start | bytes 1310720 | tf_op jit(solution)/shard_map/all_gather | solution.py:284
  10.8 174.1 %copy-start.1 = (f32[4,2]{0,1:T(2,128)S(1)}, f32[4,2]{0,1:T(2,128)}, u32[]{:S(2)}) copy-start(f32[4,2]{0,1:T(2,128)} %param.9) | copy-start | bytes 100
  10.8 174.3 %copy-start.2 = (f32[4]{0:T(128)S(1)}, f32[4]{0:T(128)}, u32[]{:S(2)}) copy-start(f32[4]{0:T(128)} %param.10) | copy-start | bytes 52
  10.8 306.0 %all-gather.8.cloned.1.call-start = ((), (), s32[]{:S(2)}) async-start(), calls=%async_computation.3 | async-start | bytes 9437184 | tf_op jit(solution)/shard_map/all_gather | solution.py:293
Sparse Core Ops, SparseCore 0:
  10.2 155.2 all-gather.5
  167.0 17.8 all-gather.3
  186.9 129.8 all-gather.7

commit v3 on v2

--- a/solution.py
+++ b/solution.py
@@ -40,7 +40,7 @@
     return vectors * lax.rsqrt(jnp.sum(vectors * vectors, axis=-1, keepdims=True) + 1e-06)
 
 
-def chunk_kernel(heads, mirrors, width, proj_ref, gate_ref, bias_ref, rate_ref, pre_ref, reach_ref, total_ref):
+def chunk_kernel(heads, mirrors, width, gate_at, proj_ref, gate_ref, bias_ref, rate_ref, pre_ref, reach_ref, total_ref):
     toks = proj_ref.shape[0]
     span = toks * mirrors
     parts = 1 + 2 * mirrors
@@ -84,10 +84,11 @@
     keys = [jnp.concatenate([unit(part(h, 1 + r)) for r in range(mirrors)], axis=0) for h in each]
     values = [jnp.concatenate([part(h, 1 + mirrors + r) for r in range(mirrors)], axis=0) for h in each]
     beta = [
-        jnp.concatenate([strength[:, h * gates + r : h * gates + r + 1] for r in range(mirrors)], axis=0)
+        jnp.concatenate([strength[:, gate_at + h * gates + r : gate_at + h * gates + r + 1] for r in range(mirrors)], axis=0)
         for h in each
     ]
-    run_q = [summed[:, h * gates + mirrors : h * gates + mirrors + 1] for h in each]
+    decay_at = [gate_at + h * gates + mirrors for h in each]
+    run_q = [summed[:, decay_at[h] : decay_at[h] + 1] for h in each]
     run = [jnp.concatenate([run_q[h]] * mirrors, axis=0) for h in each]
     run_row = [jnp.sum(jnp.where(diagonal, run[h], 0.0), axis=0, keepdims=True) for h in each]
     last = [run_q[h][toks - 1 :, :] for h in each]
@@ -123,6 +124,8 @@
         for h in each
     ]
     inv = [rough[h].astype(F32) + dot1(rough[h], left[h].astype(BF16)) for h in each]
+    left = [(eye - inv[h]) - dot3(lower[h], inv[h]) for h in each]
+    inv = [inv[h] + dot1(rough[h], left[h].astype(BF16)) for h in each]
 
     given = [
         jnp.concatenate([beta[h] * values[h], (beta[h] * jnp.exp(run[h])) * keys[h]], axis=1) for h in each
@@ -143,20 +146,21 @@
         total_ref[h, width:] = carried[width:] + moved[h][:width]
 
 
-def chunk_call(projected, gate_inputs, bias_row, rate_row, heads, mirrors, width, interpret=False):
+def chunk_call(projected, gated, bias_row, rate_row, heads, mirrors, width, first_head, interpret=False):
     toks = projected.shape[0]
     block = math.gcd(toks, BLOCK)
-    gates = gate_inputs.shape[1]
+    lanes = bias_row.shape[1]
+    gate_block = gated.shape[1] // lanes - 1
     span = block * mirrors
     units = toks // block * heads
     return pl.pallas_call(
-        functools.partial(chunk_kernel, heads, mirrors, width),
+        functools.partial(chunk_kernel, heads, mirrors, width, first_head * (mirrors + 1)),
         grid=(toks // block,),
         in_specs=[
-            pl.BlockSpec((block, projected.shape[1]), lambda i: (i, 0)),
-            pl.BlockSpec((block, gates), lambda i: (i, 0)),
-            pl.BlockSpec((1, gates), lambda i: (0, 0)),
-            pl.BlockSpec((1, gates), lambda i: (0, 0)),
+            pl.BlockSpec((block, heads * (1 + 2 * mirrors) * width), lambda i: (i, 0)),
+            pl.BlockSpec((block, lanes), lambda i: (i, gate_block)),
+            pl.BlockSpec((1, lanes), lambda i: (0, 0)),
+            pl.BlockSpec((1, lanes), lambda i: (0, 0)),
         ],
         out_specs=[
             pl.BlockSpec((block, heads * width), lambda i: (i, 0)),
@@ -173,10 +177,16 @@
             flops=2 * units * 60 * span * span * width, bytes_accessed=4 * projected.size, transcendentals=0
         ),
         interpret=interpret,
-    )(projected, gate_inputs, bias_row, rate_row)
-
-
-def relay_kernel(heads, width, pre_ref, reach_ref, total_ref, out_ref, inbox, outbox, send_sem, recv_sem):
+    )(projected, gated, bias_row, rate_row)
+
+
+def relay_kernel(heads, width, groups, *refs):
+    out_ref, inbox, outbox, send_sem, recv_sem = refs[3 * groups :]
+    each = heads // groups
+
+    def total_of(head, rows):
+        return refs[3 * (head // each) + 2][head % each, rows]
+
     me = lax.axis_index("ctx")
     group = lax.axis_index("head")
     count = lax.axis_size("ctx")
@@ -219,7 +229,7 @@
     def _():
         for head in range(heads):
             inbox[head] = jnp.zeros((width, width), F32)
-            outbox[head] = total_ref[head, width:]
+            outbox[head] = total_of(head, slice(width, None))
             copy(head).start()
 
     @pl.when(jnp.logical_not(first))
@@ -229,12 +239,16 @@
 
             @pl.when(jnp.logical_not(final))
             def _():
-                outbox[head] = dot3(inbox[head], total_ref[head, :width]) + total_ref[head, width:]
+                outbox[head] = dot3(inbox[head], total_of(head, slice(0, width))) + total_of(
+                    head, slice(width, None)
+                )
                 copy(head).start()
 
     for head in range(heads):
         cols = slice(head * width, (head + 1) * width)
-        out = pre_ref[:, cols] + dot3(reach_ref[:, cols], inbox[head], NT)
+        pre_ref, reach_ref = refs[3 * (head // each) : 3 * (head // each) + 2]
+        own = slice(head % each * width, (head % each + 1) * width)
+        out = pre_ref[:, own] + dot3(reach_ref[:, own], inbox[head], NT)
         scale = lax.rsqrt(jnp.mean(out * out, axis=-1, keepdims=True) + 1e-06)
         out_ref[:, cols] = (out * scale).astype(BF16)
 
@@ -244,11 +258,14 @@
             copy(head).wait_send()
 
 
-def relay_call(pre, reach, total, heads, width):
+def relay_call(worked, heads, width):
+    flat = [array for group in worked for array in group]
+    toks = worked[0][0].shape[0]
+    size = toks * heads * width
     return pl.pallas_call(
-        functools.partial(relay_kernel, heads, width),
-        out_shape=jax.ShapeDtypeStruct(pre.shape, BF16),
-        in_specs=[pl.BlockSpec(memory_space=pltpu.VMEM)] * 3,
+        functools.partial(relay_kernel, heads, width, len(worked)),
+        out_shape=jax.ShapeDtypeStruct((toks, heads * width), BF16),
+        in_specs=[pl.BlockSpec(memory_space=pltpu.VMEM)] * len(flat),
         out_specs=pl.BlockSpec(memory_space=pltpu.VMEM),
         scratch_shapes=[
             pltpu.VMEM((heads, width, width), F32),
@@ -260,37 +277,54 @@
             collective_id=0, has_side_effects=True, vmem_limit_bytes=32 * 2**20
         ),
         cost_estimate=pl.CostEstimate(
-            flops=6 * pre.size * width, bytes_accessed=10 * pre.size, transcendentals=0
+            flops=6 * size * width, bytes_accessed=10 * size, transcendentals=0
         ),
-    )(pre, reach, total)
+    )(*flat)
 
 
 def gate_rows(beta_bias, decay_rate):
     heads, mirrors = beta_bias.shape
+    fill = ((0, 0), (0, -heads * (mirrors + 1) % 128))
     bias = jnp.concatenate([beta_bias, jnp.zeros((heads, 1), F32)], axis=1).reshape(1, -1)
     rate = jnp.concatenate([jnp.zeros((heads, mirrors), F32), decay_rate[:, None]], axis=1).reshape(1, -1)
-    return bias, rate
+    return jnp.pad(bias, fill), jnp.pad(rate, fill)
 
 
 def shards(tokens, w_proj, w_small, beta_bias, decay_rate, w_out):
     tok_rows = tokens.shape[0]
     heads_here, mirrors = beta_bias.shape
     head_width = w_proj.shape[1] // (heads_here * (1 + 2 * mirrors))
-    wide = w_proj.shape[1]
-    fill = -w_small.shape[1] % 128
-    both = jnp.concatenate([w_proj, jnp.pad(w_small, ((0, 0), (0, fill)))], axis=1)
-    both = lax.all_gather(both, "ctx", axis=0, tiled=True)
-    projected = jnp.dot(tokens, both, preferred_element_type=F32)
-    grouped = lax.all_gather(w_out, "head", axis=0, tiled=True)
-    grouped, projected = lax.optimization_barrier((grouped, projected))
-    gate_inputs = projected[:, wide : wide + w_small.shape[1]]
-    projected = projected[:, :wide]
+    groups = math.gcd(heads_here, 2)
+    each = heads_here // groups
+    wide = w_proj.shape[1] // groups
+    small = jnp.pad(w_small, ((0, 0), (0, -w_small.shape[1] % 128)))
     bias_row, rate_row = gate_rows(beta_bias, decay_rate)
-    pre, reach, total = chunk_call(
-        projected, gate_inputs, bias_row, rate_row, heads_here, mirrors, head_width
-    )
-    mixed_heads = relay_call(pre, reach, total, heads_here, head_width)
-    full_out = lax.all_gather(grouped, "ctx", axis=1, tiled=True)
+    held = jnp.concatenate([w_proj[:, :wide], small], axis=1)
+    first_projected = None
+    worked = []
+    for group in range(groups):
+        full = lax.all_gather(held, "ctx", axis=0, tiled=True)
+        if group + 1 < groups:
+            held = w_proj[:, (group + 1) * wide : (group + 2) * wide]
+            held, w_out, full = lax.optimization_barrier((held, w_out, full))
+        if group == 0:
+            grouped = lax.all_gather(w_out, "ctx", axis=1, tiled=True)
+        else:
+            tokens, _ = lax.optimization_barrier((tokens, worked[-1][2]))
+        projected = jnp.dot(tokens, full, preferred_element_type=F32)
+        if group == 0:
+            first_projected = projected
+        if group + 1 == groups:
+            grouped, projected = lax.optimization_barrier((grouped, projected))
+            if groups == 1:
+                first_projected = projected
+        worked.append(
+            chunk_call(
+                projected, first_projected, bias_row, rate_row, each, mirrors, head_width, group * each
+            )
+        )
+    mixed_heads = relay_call(worked, heads_here, head_width)
+    full_out = lax.all_gather(grouped, "head", axis=0, tiled=True)
     group_count = lax.axis_size("head")
     rows_each = tok_rows // group_count
     stacked = mixed_heads.reshape(group_count, rows_each, heads_here * head_width)

time: 332 us -> 328 us (0.988)
  Pallas kernels: 84.9 us -> 88.7 us
    pallas_call x2 -> x3, Pallas kernels: 84.9 us -> 88.7 us  [the longest x2 55.6 us: chunk_call(): pl.pallas_call(functools.partial(chunk_kernel, heads, mirrors, width, fir...]
    slice x2 -> x1, local copies, waits for them, and re-layouts: 6.1 us -> 2.34 us  [shards(): held = jnp.concatenate([w_proj[:, :wide], small], axis=1)]
    all_gather x3 -> x4, waiting for transfers between devices: 191 us -> 188 us  [the longest x2 143 us: shards(): full = lax.all_gather(held, 'ctx', axis=0, tiled=True)]
    dot_general x1 -> x2, matrix products: 12 us -> 12.6 us  [shards(): projected = jnp.dot(tokens, full, preferred_element_type=F32)]
  transfers between devices with their start and end apart: 3 -> 4, of which waited for: 3 -> 3; matrix products, arithmetic and copies ran while one was open for 6% -> 4% of each run, Pallas kernels for 26% -> 27%
where the time goes in v3:
time: 328 us; the launch traced here: 327 us
  waiting for transfers between devices  188 us (57%)
  Pallas kernels  88.7 us (27%)
  matrix products  18.1 us (6%)
  between operations  13.2 us (4%)
  blocking collectives  12.3 us (4%)
  local copies, waits for them, and re-layouts  5.7 us (2%)
    all_gather x2, waiting for transfers between devices, shards(): full = lax.all_gather(held, 'ctx', axis=0, tiled=True)  143 us
    pallas_call x2, Pallas kernels, chunk_call(): pl.pallas_call(functools.partial(chunk_kernel, heads, mirrors, width, fir...  55.6 us
    all_gather x1, waiting for transfers between devices, shards(): grouped = lax.all_gather(w_out, 'ctx', axis=1, tiled=True)  44.5 us
    pallas_call x1, Pallas kernels, relay_call(): pl.pallas_call(functools.partial(relay_kernel, heads, width, len(worked))...  33.2 us
    dot_general x2, matrix products, shards(): projected = jnp.dot(tokens, full, preferred_element_type=F32)  12.6 us
    all_to_all x1, blocking collectives, shards(): lax.all_to_all(stacked, 'head', split_axis=0, concat_axis=2, tiled=True)  12.3 us
  transfers between devices with their start and end apart: 4, of which 3 were waited for; matrix products, arithmetic and copies ran while one was open for 4% of the time, Pallas kernels for 27%

profile of v3, /device:TPU:28, one launch (start us, length us, event | category | flops | bytes accessed | tf_op | source)
XLA Modules:
  0.0 327.3 jit_solution(2682870943601582102)
XLA Ops:
  6.5 0.0 copy-start
  6.5 0.0 copy-start.5
  6.5 0.0 copy-start.6
  6.5 0.0 copy-start.7
  6.5 0.0 all-gather.5.cloned.1.call-start
  6.6 2.3 fusion.2
  8.9 0.0 copy-done.5
  8.9 0.1 copy.17
  9.1 0.9 fusion.1
  10.0 0.0 all-gather.5.cloned.1.call-update
  10.0 0.0 all-gather.9.cloned.1.call-start
  10.1 90.9 %all-gather.5.cloned.1.call-done = bf16[2048,1408]{1,0:T(8,128)(2,1)} async-done(((bf16[256,1408]{1,0:T(8,128)(2,1)}), bf16[2048,1408]{1,0:T(8,128)(2,1)}) %all-gather.5.cloned.1.call-update) | async-done | bytes 5767184 | tf_op jit(solution)/shard_map/all_gather | solution.py:306
  100.9 0.0 all-gather.9.cloned.1.call-update
  101.0 0.0 all-gather.7.cloned.1.call-start
  101.0 0.7 all-gather.7.cloned.1.call-update
  101.7 0.0 all-gather.11.cloned.1.call-start
  101.7 0.0 copy-done.6
  101.8 0.1 copy.18
  101.9 0.1 reshape.17
  102.0 0.0 copy-done.7
  102.0 0.1 copy.19
  102.0 0.1 concatenate.11.clone
  102.1 0.1 reshape.18
  102.2 0.0 copy-done
  102.2 5.8 %convolution_bitcast_fusion.proj_ref.gate_ref = f32[512,1408]{1,0:T(8,128)S(1)} fusion(bf16[512,2048]{1,0:T(8,128)(2,1)S(1)} %copy-done, bf16[2048,1408]{1,0:T(8,128)(2,1)} %all-gather.5.cloned.1.call-done), kind=kOutput, calls=%fused_computation | convolution fusion | flops 2952790016 | bytes 10747904 | tf_op jit(solution)/shard_map/dot_general | solution.py:314
  108.0 0.0 copy-start.3
  108.0 27.5 %shard_map.64 = (f32[512,256]{1,0:T(8,128)S(1)}, f32[512,256]{1,0:T(8,128)S(1)}, f32[2,256,128]{2,1,0:T(8,128)S(1)}) custom-call(f32[512,1408]{1,0:T(8,128)S(1)} %convolution_bitcast_fusion.proj_ref.gate_ref, f32[512,1408]{1,0:T(8,128)S(1)} %convolution_bitcast_fusion.proj_ref.gate_ref, f32[1,128]{1,0:T(1,128)S(1)} %pad.14.bias_ref, f32[1,128]{1,0:T(1,128)S(1)} %pad.15.rate_ref), custom_call_target="tpu_custom_call" | custom-call | flops 4026531840 | bytes 2883584 | tf_op jit(solution)/shard_map/pallas_call | solution.py:156
  135.5 0.0 copy-done.3
  135.5 0.0 copy-start.1
  135.5 52.2 %all-gather.9.cloned.1.call-done = bf16[2048,1280]{1,0:T(8,128)(2,1)} async-done(((bf16[256,1280]{1,0:T(8,128)(2,1)}), bf16[2048,1280]{1,0:T(8,128)(2,1)}) %all-gather.9.cloned.1.call-update) | async-done | bytes 5242896 | tf_op jit(solution)/shard_map/all_gather | solution.py:306
  187.7 6.8 %fusion.3.proj_ref = f32[512,1280]{1,0:T(8,128)} fusion(bf16[512,2048]{1,0:T(8,128)(2,1)S(1)} %copy-done, bf16[2048,1280]{1,0:T(8,128)(2,1)} %all-gather.9.cloned.1.call-done), kind=kOutput, calls=%fused_computation.6 | convolution fusion | flops 2684354560 | bytes 9961472 | tf_op jit(solution)/shard_map/dot_general | solution.py:314
  194.5 0.0 copy-done.1
  194.5 44.5 %all-gather.7.cloned.1.call-done = bf16[512,2048]{1,0:T(8,128)(2,1)} async-done(((bf16[512,256]{1,0:T(8,128)(2,1)}), bf16[512,2048]{1,0:T(8,128)(2,1)}) %all-gather.7.cloned.1.call-update) | async-done | bytes 2097168 | tf_op jit(solution)/shard_map/all_gather | solution.py:311
  239.0 0.0 all-gather.11.cloned.1.call-update
  239.0 0.0 copy-start.4
  239.0 1.7 copy-done.4
  240.7 0.0 copy-start.2
  240.7 28.1 %shard_map.65 = (f32[512,256]{1,0:T(8,128)S(1)}, f32[512,256]{1,0:T(8,128)S(1)}, f32[2,256,128]{2,1,0:T(8,128)S(1)}) custom-call(f32[512,1280]{1,0:T(8,128)S(1)} %copy-done.4, f32[512,1408]{1,0:T(8,128)} %copy-done.3, f32[1,128]{1,0:T(1,128)S(1)} %pad.14.bias_ref, f32[1,128]{1,0:T(1,128)S(1)} %pad.15.rate_ref), custom_call_target="tpu_custom_call" | custom-call | flops 4026531840 | bytes 2621440 | tf_op jit(solution)/shard_map/pallas_call | solution.py:156
  268.9 0.0 copy-done.2
  268.9 33.2 %shard_map.66 = bf16[512,512]{1,0:T(8,128)(2,1)S(1)} custom-call(f32[512,256]{1,0:T(8,128)S(1)} %get-tuple-element.18.refs_0_, f32[512,256]{1,0:T(8,128)S(1)} %copy-done.2, f32[2,256,128]{2,1,0:T(8,128)S(1)} %get-tuple-element.20.refs_2_, f32[512,256]{1,0:T(8,128)S(1)} %get-tuple-element.25.refs_3_, f32[512,256]{1,0:T(8,128)S(1)} %get-tuple-element.26.refs_4_, ...), custom_call_target="tpu_custom_call" | custom-call | flops 201326592 | bytes 2621440 | tf_op jit(solution)/shard_map/pallas_call | solution.py:265
  302.0 1.0 copy.15
  303.0 12.3 %all_to_all.15 = bf16[4,128,512]{1,2,0:T(8,128)(2,1)S(1)} all-to-all(bf16[4,128,512]{1,2,0:T(8,128)(2,1)} %copy.15), channel_id=1, replica_groups=mesh['ctx'=8,'head'=4] {'head'}, dimensions={0} | all-to-all | bytes 1048576 | tf_op jit(solution)/shard_map/all_to_all | solution.py:333
  315.3 0.0 all-gather.11.cloned.1.call-done
  315.3 5.5 %convolution_convert_fusion = bf16[128,2048]{1,0:T(8,128)(2,1)} fusion(bf16[128,2048]{0,1:T(8,128)(2,1)S(1)} %bitcast.16, bf16[2048,2048]{1,0:T(8,128)(2,1)} %all-gather.11.cloned.1.call-done), kind=kOutput, calls=%fused_computation.1 | convolution fusion | flops 1074003968 | bytes 9437184 | tf_op jit(solution)/shard_map/irk,kd->ird/dot_general | solution.py:331
  (3 shorter events, 0.0 us)
Async XLA Ops:
  6.5 95.7 %copy-start = (bf16[512,2048]{1,0:T(8,128)(2,1)S(1)}, bf16[512,2048]{1,0:T(8,128)(2,1)}, u32[]{:S(2)}) copy-start(bf16[512,2048]{1,0:T(8,128)(2,1)} %param.6) | copy-start | bytes 6291460
  6.5 2.4 copy-start.5
  6.5 95.2 %copy-start.6 = (f32[4,2]{0,1:T(2,128)S(1)}, f32[4,2]{0,1:T(2,128)}, u32[]{:S(2)}) copy-start(f32[4,2]{0,1:T(2,128)} %param.9) | copy-start | bytes 100
  6.5 95.4 %copy-start.7 = (f32[4]{0:T(128)S(1)}, f32[4]{0:T(128)}, u32[]{:S(2)}) copy-start(f32[4]{0:T(128)} %param.10) | copy-start | bytes 52
  6.5 94.4 %all-gather.5.cloned.1.call-start = ((), (), s32[]{:S(2)}) async-start(), calls=%async_computation.1 | async-start | bytes 6488064 | tf_op jit(solution)/shard_map/all_gather | solution.py:306
  10.0 177.7 %all-gather.9.cloned.1.call-start = ((), (), s32[]{:S(2)}) async-start(), calls=%async_computation.3 | async-start | bytes 5898240 | tf_op jit(solution)/shard_map/all_gather | solution.py:306
  101.0 138.0 %all-gather.7.cloned.1.call-start = ((), (), s32[]{:S(2)}) async-start(), calls=%async_computation.2 | async-start | bytes 2359296 | tf_op jit(solution)/shard_map/all_gather | solution.py:311
  101.7 213.6 %all-gather.11.cloned.1.call-start = ((), (), s32[]{:S(2)}) async-start(), calls=%async_computation.4 | async-start | bytes 10485760 | tf_op jit(solution)/shard_map/all_gather | solution.py:327
  108.0 27.5 %copy-start.3 = (f32[512,1408]{1,0:T(8,128)}, f32[512,1408]{1,0:T(8,128)S(1)}, u32[]{:S(2)}) copy-start(f32[512,1408]{1,0:T(8,128)S(1)} %convolution_bitcast_fusion.proj_ref.gate_ref) | copy-start | bytes 8650756
  135.5 59.0 %copy-start.1 = (f32[512,256]{1,0:T(8,128)}, f32[512,256]{1,0:T(8,128)S(1)}, u32[]{:S(2)}) copy-start(f32[512,256]{1,0:T(8,128)S(1)} %get-tuple-element.19.refs_1_) | copy-start | bytes 1572868
  239.0 1.7 copy-start.4
  240.7 28.1 %copy-start.2 = (f32[512,256]{1,0:T(8,128)S(1)}, f32[512,256]{1,0:T(8,128)}, u32[]{:S(2)}) copy-start(f32[512,256]{1,0:T(8,128)} %copy-done.1) | copy-start | bytes 1572868
Sparse Core Ops, SparseCore 0:
  10.1 90.7 all-gather.4
  103.1 84.4 all-gather.8
  189.7 49.2 all-gather.6
  240.4 59.3 all-gather.10

commit v4 on v3

--- a/solution.py
+++ b/solution.py
@@ -290,11 +290,22 @@
     return jnp.pad(bias, fill), jnp.pad(rate, fill)
 
 
+def permuted_columns(block, axis):
+    count = lax.axis_size(axis)
+    me = lax.axis_index(axis)
+    rows, cols = block.shape
+    placed = lax.dynamic_update_slice(jnp.zeros((count, rows, cols), block.dtype), block[None], (me, 0, 0))
+    for by in range(1, count):
+        piece = lax.ppermute(block, axis, [(i, (i + by) % count) for i in range(count)])
+        placed = lax.dynamic_update_slice(placed, piece[None], (lax.rem(me + count - by, count), 0, 0))
+    return jnp.moveaxis(placed, 0, 1).reshape(rows, count * cols)
+
+
 def shards(tokens, w_proj, w_small, beta_bias, decay_rate, w_out):
     tok_rows = tokens.shape[0]
     heads_here, mirrors = beta_bias.shape
     head_width = w_proj.shape[1] // (heads_here * (1 + 2 * mirrors))
-    groups = math.gcd(heads_here, 2)
+    groups = 1
     each = heads_here // groups
     wide = w_proj.shape[1] // groups
     small = jnp.pad(w_small, ((0, 0), (0, -w_small.shape[1] % 128)))
@@ -308,7 +319,7 @@
             held = w_proj[:, (group + 1) * wide : (group + 2) * wide]
             held, w_out, full = lax.optimization_barrier((held, w_out, full))
         if group == 0:
-            grouped = lax.all_gather(w_out, "ctx", axis=1, tiled=True)
+            grouped = permuted_columns(w_out, "ctx")
         else:
             tokens, _ = lax.optimization_barrier((tokens, worked[-1][2]))
         projected = jnp.dot(tokens, full, preferred_element_type=F32)

time: 328 us -> 305 us (0.930)
  Pallas kernels: 88.7 us -> 65.1 us
  waiting for transfers between devices: 188 us -> 174 us
  starting transfers between devices: 0.15 us -> 7.81 us
  local copies, waits for them, and re-layouts: 5.7 us -> 10.8 us
    ppermute x0 -> x7, waiting for transfers between devices: none -> 72 us  [permuted_columns(): lax.ppermute(block, axis, [(i, (i + by) % count) for i in range(count)])]
    all_gather x1 -> x0, waiting for transfers between devices: 44.5 us -> none  [shards(): grouped = lax.all_gather(w_out, 'ctx', axis=1, tiled=True)]
    all_gather x2 -> x1, waiting for transfers between devices: 143 us -> 102 us  [shards(): full = lax.all_gather(held, 'ctx', axis=0, tiled=True)]
    pallas_call x2 -> x1, Pallas kernels: 55.6 us -> 33.4 us  [chunk_call(): pl.pallas_call(functools.partial(chunk_kernel, heads, mirrors, width, fir...]
    ppermute x0 -> x7, starting transfers between devices: none -> 7.77 us  [permuted_columns(): lax.ppermute(block, axis, [(i, (i + by) % count) for i in range(count)])]
    dynamic_update_slice x0 -> x8, local copies, waits for them, and re-layouts: none -> 6.74 us  [the longest x7 6.02 us: permuted_columns(): lax.dynamic_update_slice(placed, piece[None], (lax.rem(me + count - by, c...]
    dot_general x2 -> x1, matrix products: 12.6 us -> 11.9 us  [shards(): projected = jnp.dot(tokens, full, preferred_element_type=F32)]
  transfers between devices with their start and end apart: 4 -> 9, of which waited for: 3 -> 5; matrix products, arithmetic and copies ran while one was open for 4% -> 3% of each run, Pallas kernels for 27% -> 21%
where the time goes in v4:
time: 305 us; the launch traced here: 304 us
  waiting for transfers between devices  174 us (57%)
  Pallas kernels  65.1 us (21%)
  matrix products  19 us (6%)
  between operations  13.5 us (4%)
  blocking collectives  11.4 us (4%)
  local copies, waits for them, and re-layouts  10.8 us (4%)
  starting transfers between devices  7.81 us (3%)
    all_gather x1, waiting for transfers between devices, shards(): full = lax.all_gather(held, 'ctx', axis=0, tiled=True)  102 us
    ppermute x7, waiting for transfers between devices, permuted_columns(): lax.ppermute(block, axis, [(i, (i + by) % count) for i in range(count)])  72 us
    pallas_call x1, Pallas kernels, chunk_call(): pl.pallas_call(functools.partial(chunk_kernel, heads, mirrors, width, fir...  33.4 us
    pallas_call x1, Pallas kernels, relay_call(): pl.pallas_call(functools.partial(relay_kernel, heads, width, len(worked))...  31.8 us
    dot_general x1, matrix products, shards(): projected = jnp.dot(tokens, full, preferred_element_type=F32)  11.9 us
    all_to_all x1, blocking collectives, shards(): lax.all_to_all(stacked, 'head', split_axis=0, concat_axis=2, tiled=True)  11.4 us
    ppermute x7, starting transfers between devices, permuted_columns(): lax.ppermute(block, axis, [(i, (i + by) % count) for i in range(count)])  7.77 us
    dot_general x1, matrix products, shards(): jnp.einsum('irk,kd->ird', lax.all_to_all(stacked, 'head', split_axis=0, c...  7.09 us
  transfers between devices with their start and end apart: 9, of which 5 were waited for; matrix products, arithmetic and copies ran while one was open for 3% of the time, Pallas kernels for 21%

profile of v4, /device:TPU:28, one launch (start us, length us, event | category | flops | bytes accessed | tf_op | source)
XLA Modules:
  0.0 304.4 jit_solution(16917094401024408928)
XLA Ops:
  6.5 0.0 copy-start
  6.5 0.0 copy-start.1
  6.5 0.0 all-gather.3.cloned.1.call-start
  6.5 1.0 copy.25
  7.5 2.5 fusion.1
  10.0 0.0 all-gather.3.cloned.1.call-update
  10.1 0.0 all-gather.5.cloned.1.call-start
  10.1 0.0 copy-done.1
  10.1 0.1 copy.11
  10.3 0.1 collective-permute-start
  10.3 1.7 collective-permute-start.1
  12.1 1.6 collective-permute-start.2
  13.7 1.2 collective-permute-start.3
  14.9 1.7 collective-permute-start.4
  16.7 1.5 broadcast_in_dim.30
  18.2 0.7 bitcast_dynamic-update-slice_fusion.7
  18.9 0.0 collective-permute-done
  18.9 1.4 collective-permute-start.5
  20.3 1.7 bitcast_dynamic-update-slice_fusion.6
  22.0 6.4 %collective-permute-done.1 = bf16[512,256]{0,1:T(8,128)(2,1)S(1)} collective-permute-done((bf16[512,256]{0,1:T(8,128)(2,1)S(1)}, bf16[512,256]{0,1:T(8,128)(2,1)S(1)}, u32[]{:S(2)}, u32[]{:S(2)}) %collective-permute-start.1) | collective-permute-done | bytes 262176 | tf_op jit(solution)/shard_map/ppermute | solution.py:299
  28.4 0.0 collective-permute-start.6
  28.4 0.7 bitcast_dynamic-update-slice_fusion.5
  29.1 6.2 %collective-permute-done.2 = bf16[512,256]{0,1:T(8,128)(2,1)S(1)} collective-permute-done((bf16[512,256]{0,1:T(8,128)(2,1)S(1)}, bf16[512,256]{0,1:T(8,128)(2,1)S(1)}, u32[]{:S(2)}, u32[]{:S(2)}) %collective-permute-start.2) | collective-permute-done | bytes 262176 | tf_op jit(solution)/shard_map/ppermute | solution.py:299
  35.3 0.7 bitcast_dynamic-update-slice_fusion.4
  36.1 57.2 %collective-permute-done.3 = bf16[512,256]{0,1:T(8,128)(2,1)S(1)} collective-permute-done((bf16[512,256]{0,1:T(8,128)(2,1)S(1)}, bf16[512,256]{0,1:T(8,128)(2,1)S(1)}, u32[]{:S(2)}, u32[]{:S(2)}) %collective-permute-start.3) | collective-permute-done | bytes 262176 | tf_op jit(solution)/shard_map/ppermute | solution.py:299
  93.3 0.7 bitcast_dynamic-update-slice_fusion.3
  94.0 2.2 collective-permute-done.4
  96.2 0.7 bitcast_dynamic-update-slice_fusion.2
  96.9 0.0 collective-permute-done.5
  96.9 0.7 bitcast_dynamic-update-slice_fusion.1
  97.6 0.0 collective-permute-done.6
  97.6 0.7 bitcast_dynamic-update-slice_fusion
  98.4 102.2 %all-gather.3.cloned.1.call-done = bf16[2048,2688]{1,0:T(8,128)(2,1)} async-done(((bf16[256,2688]{1,0:T(8,128)(2,1)}), bf16[2048,2688]{1,0:T(8,128)(2,1)}) %all-gather.3.cloned.1.call-update) | async-done | bytes 11010064 | tf_op jit(solution)/shard_map/all_gather | solution.py:317
  200.6 0.0 copy-done
  200.6 11.9 %convolution_bitcast_fusion.proj_ref.gate_ref = f32[512,2688]{1,0:T(8,128)} fusion(bf16[512,2048]{1,0:T(8,128)(2,1)S(1)} %copy-done, bf16[2048,2688]{1,0:T(8,128)(2,1)} %all-gather.3.cloned.1.call-done), kind=kOutput, calls=%fused_computation | convolution fusion | flops 5637144576 | bytes 18612224 | tf_op jit(solution)/shard_map/dot_general | solution.py:325
  212.5 0.0 copy-start.2
  212.6 0.0 copy-start.3
  212.6 0.0 all-gather.5.cloned.1.call-update
  212.6 0.7 copy-done.2
  213.2 0.1 copy.26
  213.3 0.1 reshape.21
  213.4 0.0 copy-done.3
  213.4 0.1 copy.27
  213.5 0.1 concatenate.11.clone
  213.6 0.1 reshape.22
  213.7 33.4 %shard_map.64 = (f32[512,512]{1,0:T(8,128)S(1)}, f32[512,512]{1,0:T(8,128)S(1)}, f32[4,256,128]{2,1,0:T(8,128)S(1)}) custom-call(f32[512,2688]{1,0:T(8,128)} %convolution_bitcast_fusion.proj_ref.gate_ref, f32[512,2688]{1,0:T(8,128)} %convolution_bitcast_fusion.proj_ref.gate_ref, f32[1,128]{1,0:T(1,128)S(1)} %pad.14.bias_ref, f32[1,128]{1,0:T(1,128)S(1)} %pad.15.rate_ref), custom_call_target="tpu_custom_call" | custom-call | flops 8053063680 | bytes 5505024 | tf_op jit(solution)/shard_map/pallas_call | solution.py:156
  247.1 31.8 %shard_map.65 = bf16[512,512]{1,0:T(8,128)(2,1)S(1)} custom-call(f32[512,512]{1,0:T(8,128)S(1)} %get-tuple-element.11.refs_0_, f32[512,512]{1,0:T(8,128)S(1)} %get-tuple-element.12.refs_1_, f32[4,256,128]{2,1,0:T(8,128)S(1)} %get-tuple-element.13.refs_2_), custom_call_target="tpu_custom_call" | custom-call | flops 201326592 | bytes 2621440 | tf_op jit(solution)/shard_map/pallas_call | solution.py:265
  278.9 0.3 copy.23
  279.1 11.4 %all_to_all.15 = bf16[4,128,512]{1,2,0:T(8,128)(2,1)S(1)} all-to-all(bf16[4,128,512]{1,2,0:T(8,128)(2,1)S(1)} %copy.23), channel_id=1, replica_groups=mesh['ctx'=8,'head'=4] {'head'}, dimensions={0} | all-to-all | bytes 1048576 | tf_op jit(solution)/shard_map/all_to_all | solution.py:344
  290.5 0.0 all-gather.5.cloned.1.call-done
  290.5 7.1 %convolution_convert_fusion = bf16[128,2048]{1,0:T(8,128)(2,1)} fusion(bf16[128,2048]{0,1:T(8,128)(2,1)S(1)} %bitcast.33, bf16[2048,2048]{0,1:T(8,128)(2,1)} %all-gather.5.cloned.1.call-done), kind=kOutput, calls=%fused_computation.3 | convolution fusion | flops 1074003968 | bytes 9437184 | tf_op jit(solution)/shard_map/irk,kd->ird/dot_general | solution.py:342
  (3 shorter events, 0.0 us)
Async XLA Ops:
  6.5 194.1 %copy-start = (bf16[512,2048]{1,0:T(8,128)(2,1)S(1)}, bf16[512,2048]{1,0:T(8,128)(2,1)}, u32[]{:S(2)}) copy-start(bf16[512,2048]{1,0:T(8,128)(2,1)} %param.6) | copy-start | bytes 6291460
  6.5 3.6 %copy-start.1 = (bf16[512,256]{1,0:T(8,128)(2,1)S(1)}, bf16[512,256]{1,0:T(8,128)(2,1)}, u32[]{:S(2)}) copy-start(bf16[512,256]{1,0:T(8,128)(2,1)} %param.11) | copy-start | bytes 786436
  6.5 194.1 %all-gather.3.cloned.1.call-start = ((), (), s32[]{:S(2)}) async-start(), calls=%async_computation.1 | async-start | bytes 12386304 | tf_op jit(solution)/shard_map/all_gather | solution.py:317
  10.1 280.4 %all-gather.5.cloned.1.call-start = ((), (), s32[]{:S(2)}) async-start(), calls=%async_computation.2 | async-start | bytes 10485760 | tf_op jit(solution)/shard_map/all_gather | solution.py:338
  10.3 8.7 %collective-permute-start = (bf16[512,256]{0,1:T(8,128)(2,1)S(1)}, bf16[512,256]{0,1:T(8,128)(2,1)}, u32[]{:S(2)}, u32[]{:S(2)}) collective-permute-start(bf16[512,256]{0,1:T(8,128)(2,1)S(1)} %copy.11), channel_id=1, source_target_pairs={{0,4},{4,8},{8,12},{12,16},{16,20},{20,24},{24,28},{28,0},{1,5},{5... | collective-permute-start | bytes 786440 | tf_op jit(solution)/shard_map/ppermute | solution.py:299
  10.3 18.0 %collective-permute-start.1 = (bf16[512,256]{0,1:T(8,128)(2,1)S(1)}, bf16[512,256]{0,1:T(8,128)(2,1)S(1)}, u32[]{:S(2)}, u32[]{:S(2)}) collective-permute-start(bf16[512,256]{0,1:T(8,128)(2,1)S(1)} %copy.11), channel_id=1, source_target_pairs={{0,8},{4,12},{8,16},{12,20},{16,24},{20,28},{24,0},{28,4},{1,9},{5... | collective-permute-start | bytes 786440 | tf_op jit(solution)/shard_map/ppermute | solution.py:299
  12.1 23.2 %collective-permute-start.2 = (bf16[512,256]{0,1:T(8,128)(2,1)S(1)}, bf16[512,256]{0,1:T(8,128)(2,1)S(1)}, u32[]{:S(2)}, u32[]{:S(2)}) collective-permute-start(bf16[512,256]{0,1:T(8,128)(2,1)S(1)} %copy.11), channel_id=1, source_target_pairs={{0,12},{4,16},{8,20},{12,24},{16,28},{20,0},{24,4},{28,8},{1,13},{... | collective-permute-start | bytes 786440 | tf_op jit(solution)/shard_map/ppermute | solution.py:299
  13.7 79.6 %collective-permute-start.3 = (bf16[512,256]{0,1:T(8,128)(2,1)S(1)}, bf16[512,256]{0,1:T(8,128)(2,1)S(1)}, u32[]{:S(2)}, u32[]{:S(2)}) collective-permute-start(bf16[512,256]{0,1:T(8,128)(2,1)S(1)} %copy.11), channel_id=1, source_target_pairs={{0,16},{4,20},{8,24},{12,28},{16,0},{20,4},{24,8},{28,12},{1,17},{... | collective-permute-start | bytes 786440 | tf_op jit(solution)/shard_map/ppermute | solution.py:299
  14.9 81.3 %collective-permute-start.4 = (bf16[512,256]{0,1:T(8,128)(2,1)S(1)}, bf16[512,256]{0,1:T(8,128)(2,1)S(1)}, u32[]{:S(2)}, u32[]{:S(2)}) collective-permute-start(bf16[512,256]{0,1:T(8,128)(2,1)S(1)} %copy.11), channel_id=1, source_target_pairs={{0,20},{4,24},{8,28},{12,0},{16,4},{20,8},{24,12},{28,16},{1,21},{... | collective-permute-start | bytes 786440 | tf_op jit(solution)/shard_map/ppermute | solution.py:299
  18.9 78.0 %collective-permute-start.5 = (bf16[512,256]{0,1:T(8,128)(2,1)S(1)}, bf16[512,256]{0,1:T(8,128)(2,1)S(1)}, u32[]{:S(2)}, u32[]{:S(2)}) collective-permute-start(bf16[512,256]{0,1:T(8,128)(2,1)S(1)} %copy.11), channel_id=1, source_target_pairs={{0,24},{4,28},{8,0},{12,4},{16,8},{20,12},{24,16},{28,20},{1,25},{... | collective-permute-start | bytes 786440 | tf_op jit(solution)/shard_map/ppermute | solution.py:299
  28.4 69.3 %collective-permute-start.6 = (bf16[512,256]{0,1:T(8,128)(2,1)S(1)}, bf16[512,256]{0,1:T(8,128)(2,1)S(1)}, u32[]{:S(2)}, u32[]{:S(2)}) collective-permute-start(bf16[512,256]{0,1:T(8,128)(2,1)S(1)} %copy.11), channel_id=1, source_target_pairs={{0,28},{4,0},{8,4},{12,8},{16,12},{20,16},{24,20},{28,24},{1,29},{... | collective-permute-start | bytes 786440 | tf_op jit(solution)/shard_map/ppermute | solution.py:299
  212.5 0.7 copy-start.2
  212.6 0.9 copy-start.3
Sparse Core Ops, SparseCore 0:
  10.2 190.3 all-gather.2
  212.7 59.3 all-gather.4
